TPU v7x, 32 devices: a whole 2x2x4 slice. The times are simulated.
32 devices in a mesh: group: 2 (over core), ctx: 16 (over z, y, x).
Axes of the slice: x: 2, y: 2, z: 4, core: 2. Of those that a mesh axis runs over, the one named last changes fastest.
Arguments:
- queries: bfloat16 [512, 4096], P(('group', 'ctx')), may hold values from -16 to 16
- key_states: bfloat16 [512, 4096], P(('group', 'ctx')), may hold values from -16 to 16
- value_states: bfloat16 [512, 4096], P(('group', 'ctx')), may hold values from -6 to 6
- gate_table: float32 [32, 4096], replicated, may hold values from 0.3 to 3
- noise_levels: int32 [2], replicated, may hold values from 0 to 31
- group_ids: int32 [2], replicated, may hold values from 0 to 1, each once
Outputs:
- handed: bfloat16 [512, 4096], P(('group', 'ctx'))
Inputs may be any that keep to these rules, and one draw needn't show every extreme that they name: `group_ids`: each of 0 to 1 appears once.
All inputs are finite; a program needn't handle non-finite values.
Results may differ from a plain program's by a relative error of at most 0.007.
Values may be sent and summed in bfloat16 or wider, within the bound.
No kernel may reach another device: no remote copies, remote signals or barrier semaphores. Data moves between devices by JAX's collectives and lax.ppermute only.
A program may use at most 64 MiB of HBM per device.

v0:
```python
import jax
import jax.numpy as jnp
from jax import lax
from jax.sharding import PartitionSpec as P

HEADS = 32
HEAD = 128


def shifted(block, axis, distance):
    devices = range(lax.axis_size(axis))
    route = [((i - distance) % len(devices), i) for i in devices]
    return lax.ppermute(block, axis, route)


def doubled(states):
    row_count = states.shape[0]
    shaped = states.reshape(row_count, HEADS, 1, HEAD)
    return jnp.broadcast_to(shaped, (row_count, HEADS, 2, HEAD)).reshape(row_count, 2 * HEADS, HEAD)


def attend(running, chosen, key_block, value_block, key_group, group_ids, own_id):
    peak, total, summed = running
    marked = key_group[:, None] == jnp.arange(group_ids.shape[0], dtype=jnp.int32)[None, :]
    key_ids = jnp.sum(jnp.where(marked, group_ids[None, :], 0), axis=1)
    allowed = (key_ids <= own_id)[None, None, :]
    scores = jnp.einsum("pqd,rpd->pqr", chosen, key_block, preferred_element_type=jnp.float32)
    scores = jnp.where(allowed, scores * (1.0 / HEAD**0.5), -1e30)
    new_peak = jnp.maximum(peak, jnp.max(scores, axis=-1))
    weights = jnp.where(allowed, jnp.exp(scores - new_peak[..., None]), 0.0)
    total = jnp.sum(weights, axis=-1)
    summed = jnp.einsum(
        "pqr,rpd->pqd",
        weights.astype(jnp.bfloat16),
        value_block,
        preferred_element_type=jnp.float32,
    )
    return (new_peak, total, summed)


def local(queries, key_states, value_states, gate_table, noise_levels, group_ids):
    tok_count = queries.shape[0]
    ctx_count = lax.axis_size("ctx")
    group_count = lax.axis_size("group")
    slot_count = 2 * HEADS // ctx_count
    group_rows = tok_count * ctx_count
    half_rows = group_rows // 2
    section_marks = jnp.arange(group_count, dtype=jnp.int32) == lax.axis_index("group")
    own_id = jnp.sum(jnp.where(section_marks, group_ids, 0))
    own_level = jnp.sum(jnp.where(section_marks, noise_levels, 0))
    slot_index = lax.axis_index("ctx") * slot_count + jnp.arange(slot_count, dtype=jnp.int32)
    offsets = slot_index % 2 * half_rows

    def select(offset, block):
        return lax.dynamic_slice_in_dim(block, offset, half_rows, 0)

    initial = (
        jnp.full((slot_count, half_rows), -1e30, jnp.float32),
        jnp.zeros((slot_count, half_rows), jnp.float32),
        jnp.zeros((slot_count, half_rows, HEAD), jnp.float32),
    )
    query_heads, key_heads, value_heads = (
        lax.all_to_all(doubled(queries), "ctx", split_axis=1, concat_axis=0, tiled=True),
        lax.all_to_all(doubled(key_states), "ctx", split_axis=1, concat_axis=0, tiled=True),
        lax.all_to_all(doubled(value_states), "ctx", split_axis=1, concat_axis=0, tiled=True),
    )
    chosen = jax.vmap(select, in_axes=(0, 1))(offsets, query_heads)
    key_piece = lax.all_gather(key_heads, "group", axis=0, tiled=True)
    value_piece = lax.all_gather(value_heads, "group", axis=0, tiled=True)
    key_group = jnp.arange(key_piece.shape[0], dtype=jnp.int32) // group_rows
    running = attend(initial, chosen, key_piece, value_piece, key_group, group_ids, own_id)
    peak, total, summed = running
    attended = (summed / total[..., None]).astype(jnp.bfloat16)

    def place(offset, block):
        return lax.dynamic_update_slice_in_dim(
            jnp.zeros((group_rows, HEAD), jnp.bfloat16), block, offset, 0
        )

    spread = jax.vmap(place, out_axes=1)(offsets, attended)
    returned = lax.all_to_all(spread, "ctx", split_axis=0, concat_axis=1, tiled=True)
    paired = returned.reshape(tok_count, HEADS, 2, HEAD)
    merged = (paired[:, :, 0] + paired[:, :, 1]).reshape(tok_count, HEADS * HEAD)
    level_marks = jnp.arange(gate_table.shape[0], dtype=jnp.int32)[:, None] == own_level
    gate_row = jnp.sum(jnp.where(level_marks, gate_table, 0.0), axis=0)
    done = (merged.astype(jnp.float32) * gate_row[None, :]).astype(jnp.bfloat16)
    return shifted(done, "group", 1)


def solution(mesh):
    placed = (
        P(("group", "ctx"), None),
        P(("group", "ctx"), None),
        P(("group", "ctx"), None),
        P(),
        P(),
        P(),
    )
    return jax.shard_map(
        local, mesh=mesh, in_specs=placed, out_specs=P(("group", "ctx"), None), check_vma=False
    )
```

profile of v0, /device:TPU:1, one launch (start us, length us, event | category | flops | bytes accessed | tf_op | source)
XLA Modules:
  0.0 94.5 jit_solution(1286835427834205812)
XLA Ops:
  1.7 7.5 %all-to-all-start = ((bf16[16,64,128]{2,0,1:T(8,128)(2,1)}), bf16[16,64,128]{2,0,1:T(8,128)(2,1)S(1)}, u32[]{:S(2)}, u32[]{:S(2)}) async-start(bf16[16,64,128]{2,0,1:T(8,128)(2,1)} %bitcast), calls=%async_computation | async-start | bytes 524288 | tf_op jit(solution)/shard_map/all_to_all | solution.py:63
  11.4 5.8 %all-to-all-done = bf16[16,64,128]{2,0,1:T(8,128)(2,1)S(1)} async-done(((bf16[16,64,128]{2,0,1:T(8,128)(2,1)}), bf16[16,64,128]{2,0,1:T(8,128)(2,1)S(1)}, u32[]{:S(2)}, u32[]{:S(2)}) %all-to-all-start) | async-done | bytes 262176 | tf_op jit(solution)/shard_map/all_to_all | solution.py:63
  17.9 4.9 %all-to-all-start.1 = ((bf16[16,64,128]{2,0,1:T(8,128)(2,1)}), bf16[16,64,128]{2,0,1:T(8,128)(2,1)S(1)}, u32[]{:S(2)}, u32[]{:S(2)}) async-start(bf16[16,64,128]{2,0,1:T(8,128)(2,1)} %bitcast.5), calls=%async_computation.1 | async-start | bytes 524288 | tf_op jit(solution)/shard_map/all_to_all | solution.py:64
  23.9 6.5 %all-to-all-done.1 = bf16[16,64,128]{2,0,1:T(8,128)(2,1)S(1)} async-done(((bf16[16,64,128]{2,0,1:T(8,128)(2,1)}), bf16[16,64,128]{2,0,1:T(8,128)(2,1)S(1)}, u32[]{:S(2)}, u32[]{:S(2)}) %all-to-all-start.1) | async-done | bytes 262176 | tf_op jit(solution)/shard_map/all_to_all | solution.py:64
  31.1 5.2 %all-to-all-start.2 = ((bf16[16,64,128]{2,0,1:T(8,128)(2,1)}), bf16[16,64,128]{2,0,1:T(8,128)(2,1)S(1)}, u32[]{:S(2)}, u32[]{:S(2)}) async-start(bf16[16,64,128]{2,0,1:T(8,128)(2,1)} %bitcast.9), calls=%async_computation.2 | async-start | bytes 524288 | tf_op jit(solution)/shard_map/all_to_all | solution.py:65
  36.3 3.5 %all_gather.6 = bf16[512,4,128]{2,0,1:T(8,128)(2,1)S(1)} all-gather(bf16[256,4,128]{2,0,1:T(8,128)(2,1)S(1)} %bitcast.64), channel_id=1, replica_groups=mesh['group'=2,'ctx'=16] {'group'}, dimensions={0}, use_global_device_ids=true | all-gather | bytes 786432 | tf_op jit(solution)/shard_map/all_gather | solution.py:68
  41.4 2.4 %all-to-all-done.2 = bf16[16,64,128]{2,0,1:T(8,128)(2,1)S(1)} async-done(((bf16[16,64,128]{2,0,1:T(8,128)(2,1)}), bf16[16,64,128]{2,0,1:T(8,128)(2,1)S(1)}, u32[]{:S(2)}, u32[]{:S(2)}) %all-to-all-start.2) | async-done | bytes 262176 | tf_op jit(solution)/shard_map/all_to_all | solution.py:65
  43.8 5.1 %all_gather.7 = bf16[512,4,128]{2,0,1:T(8,128)(2,1)S(1)} all-gather(bf16[256,4,128]{2,0,1:T(8,128)(2,1)S(1)} %bitcast.65), channel_id=1, replica_groups=mesh['group'=2,'ctx'=16] {'group'}, dimensions={0}, use_global_device_ids=true | all-gather | bytes 786432 | tf_op jit(solution)/shard_map/all_gather | solution.py:69
  50.3 26.9 %while.1 = (s32[]{:T(128)}, bf16[4,256,128]{2,1,0:T(8,128)(2,1)S(1)}, s32[4,3]{1,0:T(4,128)S(1)}, bf16[4,128,128]{2,1,0:T(8,128)(2,1)S(1)}, s32[]{:T(128)}, /*index=5*/s32[3]{0:T(128)S(1)}, s32[]{:T(128)}) while((s32[]{:T(128)}, bf16[4,256,128]{2,1,0:T(8,128)(2,1)S(1)}, s32[4,3]{1,0:T(4,128)S(1)}, bf16[4,128,128]{2,1,0:T(8,128)(2,1)S(1)}, s32[]{:T(128)}, ...), condition=%wide.while_cond, body=%wide.while_body.sunk | while | flops 16403 | bytes 164011 | solution.py:76
  50.9 2.7 %and_reduce_fusion.2 = pred[]{:T(512)} fusion(s32[3]{0:T(128)S(1)} %get-tuple-element.76, s32[1]{0:T(128)} %bitcast.60, s32[1]{0:T(128)} %bitcast.61, s32[1]{0:T(128)} %bitcast.62), kind=kLoop, calls=%fused_computation.2.clone.1 | loop fusion | flops 17 | bytes 25 | tf_op jit(solution)/shard_map/vmap(vmap())/scatter
  53.6 1.9 %dynamic-slice_select_fusion.2 = bf16[1,128,128]{2,1,0:T(8,128)(2,1)S(1)} fusion(bf16[4,128,128]{2,1,0:T(8,128)(2,1)S(1)} %get-tuple-element.74, s32[]{:T(128)} %get-tuple-element.64, bf16[4,256,128]{2,1,0:T(8,128)(2,1)S(1)} %get-tuple-element.65, s32[]{:T(128)} %bitcast.58, s32[]{:T(128)} %bitcast.59, pred[]{:T(512)} %and_reduce_fusion.2), kind=kLoop, calls=%fused_computation.1.clone.1 | loop fusion | flops 16384 | bytes 98317 | tf_op jit(solution)/shard_map/vmap(vmap())/scatter
  55.5 1.5 %dynamic-update-slice.3 = bf16[4,256,128]{2,1,0:T(8,128)(2,1)S(1)} dynamic-update-slice(bf16[4,256,128]{2,1,0:T(8,128)(2,1)S(1)} %get-tuple-element.65, bf16[1,128,128]{2,1,0:T(8,128)(2,1)S(1)} %dynamic-slice_select_fusion.2, s32[]{:T(128)} %bitcast.58, s32[]{:T(128)} %bitcast.59, s32[]{:T(128)} %constant.25.clone.1..sunk) | dynamic-update-slice | bytes 65540 | tf_op jit(solution)/shard_map/vmap(vmap())/scatter
  57.7 2.7 %and_reduce_fusion.2 = pred[]{:T(512)} fusion(s32[3]{0:T(128)S(1)} %get-tuple-element.76, s32[1]{0:T(128)} %bitcast.60, s32[1]{0:T(128)} %bitcast.61, s32[1]{0:T(128)} %bitcast.62), kind=kLoop, calls=%fused_computation.2.clone.1 | loop fusion | flops 17 | bytes 25 | tf_op jit(solution)/shard_map/vmap(vmap())/scatter
  60.3 1.9 %dynamic-slice_select_fusion.2 = bf16[1,128,128]{2,1,0:T(8,128)(2,1)S(1)} fusion(bf16[4,128,128]{2,1,0:T(8,128)(2,1)S(1)} %get-tuple-element.74, s32[]{:T(128)} %get-tuple-element.64, bf16[4,256,128]{2,1,0:T(8,128)(2,1)S(1)} %get-tuple-element.65, s32[]{:T(128)} %bitcast.58, s32[]{:T(128)} %bitcast.59, pred[]{:T(512)} %and_reduce_fusion.2), kind=kLoop, calls=%fused_computation.1.clone.1 | loop fusion | flops 16384 | bytes 98317 | tf_op jit(solution)/shard_map/vmap(vmap())/scatter
  62.2 1.4 %dynamic-update-slice.3 = bf16[4,256,128]{2,1,0:T(8,128)(2,1)S(1)} dynamic-update-slice(bf16[4,256,128]{2,1,0:T(8,128)(2,1)S(1)} %get-tuple-element.65, bf16[1,128,128]{2,1,0:T(8,128)(2,1)S(1)} %dynamic-slice_select_fusion.2, s32[]{:T(128)} %bitcast.58, s32[]{:T(128)} %bitcast.59, s32[]{:T(128)} %constant.25.clone.1..sunk) | dynamic-update-slice | bytes 65540 | tf_op jit(solution)/shard_map/vmap(vmap())/scatter
  64.4 2.7 %and_reduce_fusion.2 = pred[]{:T(512)} fusion(s32[3]{0:T(128)S(1)} %get-tuple-element.76, s32[1]{0:T(128)} %bitcast.60, s32[1]{0:T(128)} %bitcast.61, s32[1]{0:T(128)} %bitcast.62), kind=kLoop, calls=%fused_computation.2.clone.1 | loop fusion | flops 17 | bytes 25 | tf_op jit(solution)/shard_map/vmap(vmap())/scatter
  67.0 1.9 %dynamic-slice_select_fusion.2 = bf16[1,128,128]{2,1,0:T(8,128)(2,1)S(1)} fusion(bf16[4,128,128]{2,1,0:T(8,128)(2,1)S(1)} %get-tuple-element.74, s32[]{:T(128)} %get-tuple-element.64, bf16[4,256,128]{2,1,0:T(8,128)(2,1)S(1)} %get-tuple-element.65, s32[]{:T(128)} %bitcast.58, s32[]{:T(128)} %bitcast.59, pred[]{:T(512)} %and_reduce_fusion.2), kind=kLoop, calls=%fused_computation.1.clone.1 | loop fusion | flops 16384 | bytes 98317 | tf_op jit(solution)/shard_map/vmap(vmap())/scatter
  68.9 1.5 %dynamic-update-slice.3 = bf16[4,256,128]{2,1,0:T(8,128)(2,1)S(1)} dynamic-update-slice(bf16[4,256,128]{2,1,0:T(8,128)(2,1)S(1)} %get-tuple-element.65, bf16[1,128,128]{2,1,0:T(8,128)(2,1)S(1)} %dynamic-slice_select_fusion.2, s32[]{:T(128)} %bitcast.58, s32[]{:T(128)} %bitcast.59, s32[]{:T(128)} %constant.25.clone.1..sunk) | dynamic-update-slice | bytes 65540 | tf_op jit(solution)/shard_map/vmap(vmap())/scatter
  71.1 2.7 %and_reduce_fusion.2 = pred[]{:T(512)} fusion(s32[3]{0:T(128)S(1)} %get-tuple-element.76, s32[1]{0:T(128)} %bitcast.60, s32[1]{0:T(128)} %bitcast.61, s32[1]{0:T(128)} %bitcast.62), kind=kLoop, calls=%fused_computation.2.clone.1 | loop fusion | flops 17 | bytes 25 | tf_op jit(solution)/shard_map/vmap(vmap())/scatter
  73.7 1.9 %dynamic-slice_select_fusion.2 = bf16[1,128,128]{2,1,0:T(8,128)(2,1)S(1)} fusion(bf16[4,128,128]{2,1,0:T(8,128)(2,1)S(1)} %get-tuple-element.74, s32[]{:T(128)} %get-tuple-element.64, bf16[4,256,128]{2,1,0:T(8,128)(2,1)S(1)} %get-tuple-element.65, s32[]{:T(128)} %bitcast.58, s32[]{:T(128)} %bitcast.59, pred[]{:T(512)} %and_reduce_fusion.2), kind=kLoop, calls=%fused_computation.1.clone.1 | loop fusion | flops 16384 | bytes 98317 | tf_op jit(solution)/shard_map/vmap(vmap())/scatter
  75.7 1.4 %dynamic-update-slice.3 = bf16[4,256,128]{2,1,0:T(8,128)(2,1)S(1)} dynamic-update-slice(bf16[4,256,128]{2,1,0:T(8,128)(2,1)S(1)} %get-tuple-element.65, bf16[1,128,128]{2,1,0:T(8,128)(2,1)S(1)} %dynamic-slice_select_fusion.2, s32[]{:T(128)} %bitcast.58, s32[]{:T(128)} %bitcast.59, s32[]{:T(128)} %constant.25.clone.1..sunk) | dynamic-update-slice | bytes 65540 | tf_op jit(solution)/shard_map/vmap(vmap())/scatter
  78.0 3.7 %all-to-all-start.3 = ((bf16[256,4,128]{2,1,0:T(4,128)(2,1)}), bf16[256,4,128]{2,1,0:T(4,128)(2,1)S(1)}, u32[]{:S(2)}, u32[]{:S(2)}) async-start(bf16[256,4,128]{2,1,0:T(4,128)(2,1)} %bitcast.52), calls=%async_computation.3 | async-start | bytes 524288 | tf_op jit(solution)/shard_map/all_to_all | solution.py:81
  83.1 7.4 %all-to-all-done.3 = bf16[256,4,128]{2,1,0:T(4,128)(2,1)S(1)} async-done(((bf16[256,4,128]{2,1,0:T(4,128)(2,1)}), bf16[256,4,128]{2,1,0:T(4,128)(2,1)S(1)}, u32[]{:S(2)}, u32[]{:S(2)}) %all-to-all-start.3) | async-done | bytes 262176 | tf_op jit(solution)/shard_map/all_to_all | solution.py:81
  90.9 2.0 %collective-permute-start = (bf16[16,4096]{1,0:T(8,128)(2,1)S(1)}, bf16[16,4096]{1,0:T(8,128)(2,1)S(1)}, u32[]{:S(2)}, u32[]{:S(2)}) collective-permute-start(bf16[16,4096]{1,0:T(8,128)(2,1)S(1)} %fusion.8), channel_id=1, source_target_pairs={{16,0},{0,16},{17,1},{1,17},{18,2},{2,18},{19,3},{3,19},{20,4},{4,... | collective-permute-start | bytes 393224 | tf_op jit(solution)/shard_map/ppermute | solution.py:13
  (59 shorter events, 16.1 us)
Async XLA Ops:
  0.0 0.9 copy-start
  1.7 9.7 %copy-start.2 = (bf16[16,4096]{1,0:T(8,128)(2,1)S(1)}, bf16[16,4096]{1,0:T(8,128)(2,1)}, u32[]{:S(2)}) copy-start(bf16[16,4096]{1,0:T(8,128)(2,1)} %param.7) | copy-start | bytes 393220
  1.7 15.5 %all-to-all-start = ((bf16[16,64,128]{2,0,1:T(8,128)(2,1)}), bf16[16,64,128]{2,0,1:T(8,128)(2,1)S(1)}, u32[]{:S(2)}, u32[]{:S(2)}) async-start(bf16[16,64,128]{2,0,1:T(8,128)(2,1)} %bitcast), calls=%async_computation | async-start | bytes 524288 | tf_op jit(solution)/shard_map/all_to_all | solution.py:63
  9.2 0.7 copy-start.5
  10.7 0.7 copy-start.6
  17.9 5.8 %copy-start.3 = (bf16[16,4096]{1,0:T(8,128)(2,1)S(1)}, bf16[16,4096]{1,0:T(8,128)(2,1)}, u32[]{:S(2)}) copy-start(bf16[16,4096]{1,0:T(8,128)(2,1)} %param.8) | copy-start | bytes 393220
  17.9 12.4 %all-to-all-start.1 = ((bf16[16,64,128]{2,0,1:T(8,128)(2,1)}), bf16[16,64,128]{2,0,1:T(8,128)(2,1)S(1)}, u32[]{:S(2)}, u32[]{:S(2)}) async-start(bf16[16,64,128]{2,0,1:T(8,128)(2,1)} %bitcast.5), calls=%async_computation.1 | async-start | bytes 524288 | tf_op jit(solution)/shard_map/all_to_all | solution.py:64
  31.1 12.7 %all-to-all-start.2 = ((bf16[16,64,128]{2,0,1:T(8,128)(2,1)}), bf16[16,64,128]{2,0,1:T(8,128)(2,1)S(1)}, u32[]{:S(2)}, u32[]{:S(2)}) async-start(bf16[16,64,128]{2,0,1:T(8,128)(2,1)} %bitcast.9), calls=%async_computation.2 | async-start | bytes 524288 | tf_op jit(solution)/shard_map/all_to_all | solution.py:65
  49.6 0.7 copy-start.4
  77.1 5.9 %copy-start.1 = (f32[32,4096]{1,0:T(8,128)S(1)}, f32[32,4096]{1,0:T(8,128)}, u32[]{:S(2)}) copy-start(f32[32,4096]{1,0:T(8,128)} %param.9) | copy-start | bytes 1572868
  78.0 3.7 %copy-start.7 = (s32[2]{0:T(128)S(1)}, s32[2]{0:T(128)}, u32[]{:S(2)}) copy-start(s32[2]{0:T(128)} %param.10) | copy-start | bytes 28
  78.0 12.5 %all-to-all-start.3 = ((bf16[256,4,128]{2,1,0:T(4,128)(2,1)}), bf16[256,4,128]{2,1,0:T(4,128)(2,1)S(1)}, u32[]{:S(2)}, u32[]{:S(2)}) async-start(bf16[256,4,128]{2,1,0:T(4,128)(2,1)} %bitcast.52), calls=%async_computation.3 | async-start | bytes 524288 | tf_op jit(solution)/shard_map/all_to_all | solution.py:81
  90.9 3.0 %collective-permute-start = (bf16[16,4096]{1,0:T(8,128)(2,1)S(1)}, bf16[16,4096]{1,0:T(8,128)(2,1)S(1)}, u32[]{:S(2)}, u32[]{:S(2)}) collective-permute-start(bf16[16,4096]{1,0:T(8,128)(2,1)S(1)} %fusion.8), channel_id=1, source_target_pairs={{16,0},{0,16},{17,1},{1,17},{18,2},{2,18},{19,3},{3,19},{20,4},{4,... | collective-permute-start | bytes 393224 | tf_op jit(solution)/shard_map/ppermute | solution.py:13
where the time goes:
time: 95.7 us; the launch traced here: 94.5 us
  starting transfers between devices  23.3 us (24%)
  waiting for transfers between devices  23 us (24%)
  other arithmetic  21.7 us (23%)
  local copies, waits for them, and re-layouts  16.7 us (17%)
  blocking collectives  8.63 us (9%)
    scatter x8, other arithmetic  18.2 us
    scatter x12, local copies, waits for them, and re-layouts  8.52 us
    all_to_all x1, starting transfers between devices, local(): lax.all_to_all(doubled(queries), 'ctx', split_axis=1, concat_axis=0, tile...  7.55 us
    all_to_all x1, waiting for transfers between devices, local(): lax.all_to_all(spread, 'ctx', split_axis=0, concat_axis=1, tiled=True)  7.36 us
    all_to_all x1, waiting for transfers between devices, local(): lax.all_to_all(doubled(key_states), 'ctx', split_axis=1, concat_axis=0, t...  6.49 us
    all_to_all x1, waiting for transfers between devices, local(): lax.all_to_all(doubled(queries), 'ctx', split_axis=1, concat_axis=0, tile...  5.81 us
    all_to_all x1, starting transfers between devices, local(): lax.all_to_all(doubled(value_states), 'ctx', split_axis=1, concat_axis=0,...  5.16 us
    all_gather x1, blocking collectives, local(): value_piece = lax.all_gather(value_heads, 'group', axis=0, tiled=True)  5.12 us
  transfers between devices with their start and end apart: 5, of which 5 were waited for; matrix products, arithmetic and copies ran while one was open for 5% of the time, Pallas kernels for 0%

commit v1 on v0

--- a/solution.py
+++ b/solution.py
@@ -1,10 +1,150 @@
 import jax
 import jax.numpy as jnp
 from jax import lax
+from jax.experimental import pallas as pl
+from jax.experimental.pallas import tpu as pltpu
 from jax.sharding import PartitionSpec as P
 
 HEADS = 32
 HEAD = 128
+LOG2_E = 1.4426950408889634
+TILE = 8
+FIRST = 11
+BITS = (3, 2, 1, 0)
+
+
+def member_at(place):
+    return FIRST ^ sum((place >> bit & 1) << to for bit, to in enumerate(BITS))
+
+
+def place_of(member):
+    return sum(((member ^ FIRST) >> to & 1) << bit for bit, to in enumerate(BITS))
+
+
+def members_by_place(members):
+    return [[member_at(place) for place in range(members)]]
+
+
+def pack_kernel(
+    levels_ref, ids_ref, gate_ref, query_ref, key_ref, value_ref,
+    packed_ref, side_ref, levels, ids, gate_block, sems,
+):
+    width = gate_block.shape[1]
+    place = place_of(lax.axis_index("ctx"))
+    columns = pl.ds(pl.multiple_of(place * width, width), width)
+    pairs = [(levels_ref, levels), (ids_ref, ids), (gate_ref.at[:, columns], gate_block)]
+    for part, ref in enumerate((query_ref, key_ref, value_ref)):
+        for tile in range(ref.shape[0]):
+            pairs.append((ref.at[tile], packed_ref.at[:, part, :, tile]))
+    fetches = [pltpu.make_async_copy(*pair, sems.at[i]) for i, pair in enumerate(pairs)]
+    for fetch in fetches:
+        fetch.start()
+    for fetch in fetches[:3]:
+        fetch.wait()
+    own = lax.axis_index("group")
+    other = 1 - own
+    level_rows = lax.broadcasted_iota(jnp.int32, gate_block.shape, 0)
+    gate = jnp.sum(jnp.where(level_rows == levels[other], gate_block[...], 0.0), axis=0, keepdims=True)
+    mask = jnp.full((1, HEAD), jnp.where(ids[own] <= ids[other], 0.0, -1e30), jnp.float32)
+    parts = [gate[:, at : at + HEAD] for at in range(0, width, HEAD)]
+    side_ref[pl.ds(0, len(parts) + 1), :] = jnp.concatenate([*parts, mask], axis=0)
+    for fetch in fetches[3:]:
+        fetch.wait()
+
+
+def attend_kernel(side_ref, own_ref, other_ref, out_ref):
+    members, pair, rows, _ = out_ref.shape
+    group_rows = members * rows
+    factor = LOG2_E / HEAD**0.5
+
+    def tokens(ref, part, head):
+        return ref[:, pl.ds((part * pair + head) * rows, rows), :].reshape(group_rows, HEAD)
+
+    def dot(a, b, contract):
+        return lax.dot_general(a, b, ((contract[:1], contract[1:]), ((), ())), preferred_element_type=jnp.float32)
+
+    ones = jnp.ones((group_rows, HEAD), jnp.bfloat16)
+    mask = jnp.concatenate([side_ref[pair : pair + 1, :]] * (group_rows // HEAD), axis=1)
+    for head in range(pair):
+        queries = tokens(other_ref, 0, head)
+        scores = [dot(queries, tokens(ref, 1, head), (1, 1)) for ref in (own_ref, other_ref)]
+        scores[0] = scores[0] + mask
+        peak = jnp.max(jnp.maximum(*scores), axis=1, keepdims=True)
+        weights = [jnp.exp2((score - peak) * factor).astype(jnp.bfloat16) for score in scores]
+        values = [jnp.concatenate([tokens(ref, 2, head), ones], axis=1) for ref in (own_ref, other_ref)]
+        summed = sum(dot(weight, value, (1, 0)) for weight, value in zip(weights, values))
+        attended = (summed[:, :HEAD] / summed[:, HEAD:]).astype(jnp.bfloat16)
+        done = (attended.astype(jnp.float32) * side_ref[head : head + 1, :]).astype(jnp.bfloat16)
+        out_ref[:, head] = done.reshape(members, rows, HEAD)
+
+
+def unpack_kernel(heads_ref, out_ref, sems):
+    copies = [
+        pltpu.make_async_copy(heads_ref.at[:, :, tile], out_ref.at[tile], sems.at[tile])
+        for tile in range(out_ref.shape[0])
+    ]
+    for copy in copies:
+        copy.start()
+    for copy in copies:
+        copy.wait()
+
+
+def in_vmem(array):
+    return pltpu.with_memory_space_constraint(array, pltpu.VMEM)
+
+
+def tiled(states, members):
+    rows, columns = states.shape
+    pair = columns // HEAD // members
+    return states.reshape(rows // TILE, TILE, members, pair, HEAD).transpose(0, 2, 3, 1, 4)
+
+
+def exchanged(chunks):
+    members = members_by_place(chunks.shape[0])
+    return lax.all_to_all(chunks, "ctx", split_axis=0, concat_axis=0, tiled=True, axis_index_groups=members)
+
+
+def local(queries, key_states, value_states, gate_table, noise_levels, group_ids):
+    rows = queries.shape[0]
+    tiles = rows // TILE
+    members = lax.axis_size("ctx")
+    pair = HEADS // members
+    whole = pl.BlockSpec(memory_space=pltpu.VMEM)
+    hbm = pl.BlockSpec(memory_space=pltpu.HBM)
+    states = (tiled(array, members) for array in (queries, key_states, value_states))
+    sources = (noise_levels, group_ids, gate_table, *states)
+    packed, side = pl.pallas_call(
+        pack_kernel,
+        out_shape=[
+            pltpu.VMEM((members, 3, pair, tiles, TILE, HEAD), jnp.bfloat16),
+            pltpu.VMEM((8, HEAD), jnp.float32),
+        ],
+        in_specs=[hbm] * len(sources),
+        out_specs=[whole, whole],
+        scratch_shapes=[
+            pltpu.SMEM(noise_levels.shape, jnp.int32),
+            pltpu.SMEM(group_ids.shape, jnp.int32),
+            pltpu.VMEM((gate_table.shape[0], pair * HEAD), jnp.float32),
+            pltpu.SemaphoreType.DMA((3 + 3 * tiles,)),
+        ],
+    )(*(pltpu.with_memory_space_constraint(source, pltpu.HBM) for source in sources))
+    own = exchanged(packed.reshape(members, 3 * pair * rows, HEAD))
+    other = lax.ppermute(own, "group", [(0, 1), (1, 0)])
+    done = pl.pallas_call(
+        attend_kernel,
+        out_shape=pltpu.VMEM((members, pair, rows, HEAD), jnp.bfloat16),
+        in_specs=[whole] * 3,
+        out_specs=whole,
+    )(in_vmem(side), in_vmem(own), in_vmem(other))
+    returned = exchanged(done.reshape(members, pair * rows, HEAD))
+    handed = pl.pallas_call(
+        unpack_kernel,
+        out_shape=pltpu.HBM((tiles, members, pair, TILE, HEAD), jnp.bfloat16),
+        in_specs=[whole],
+        out_specs=hbm,
+        scratch_shapes=[pltpu.SemaphoreType.DMA((tiles,))],
+    )(in_vmem(returned.reshape(members, pair, tiles, TILE, HEAD)))
+    return handed.transpose(0, 3, 1, 2, 4).reshape(rows, HEADS * HEAD)
 
 
 def shifted(block, axis, distance):
@@ -38,7 +178,7 @@
     return (new_peak, total, summed)
 
 
-def local(queries, key_states, value_states, gate_table, noise_levels, group_ids):
+def local_wide(queries, key_states, value_states, gate_table, noise_levels, group_ids):
     tok_count = queries.shape[0]
     ctx_count = lax.axis_size("ctx")
     group_count = lax.axis_size("group")
@@ -88,14 +228,12 @@
 
 
 def solution(mesh):
-    placed = (
-        P(("group", "ctx"), None),
-        P(("group", "ctx"), None),
-        P(("group", "ctx"), None),
-        P(),
-        P(),
-        P(),
-    )
+    in_pairs = mesh.shape["group"] == 2 and 2 * mesh.shape["ctx"] == HEADS == 2 << len(BITS)
+    tokens = P(("group", "ctx"), None)
     return jax.shard_map(
-        local, mesh=mesh, in_specs=placed, out_specs=P(("group", "ctx"), None), check_vma=False
-    )
+        local if in_pairs else local_wide,
+        mesh=mesh,
+        in_specs=(tokens, tokens, tokens, P(), P(), P()),
+        out_specs=tokens,
+        check_vma=False,
+    )

time: 95.7 us -> 32.5 us (0.34)
  the two profiles are of different devices: /device:TPU:1 before, /device:TPU:0 now
where the time goes in v1:
time: 32.5 us; the launch traced here: 32.2 us
  blocking collectives  28 us (86%)
  Pallas kernels  2.47 us (8%)
  waiting for transfers between devices  1.72 us (5%)
    all_to_all x2, blocking collectives, exchanged(): lax.all_to_all(chunks, 'ctx', split_axis=0, concat_axis=0, tiled=True, ax...  28 us
    ppermute x1, waiting for transfers between devices, local(): other = lax.ppermute(own, 'group', [(0, 1), (1, 0)])  1.72 us
    pallas_call x1, Pallas kernels, local(): pl.pallas_call(pack_kernel, out_shape=[pltpu.VMEM((members, 3, pair, tile...  1.09 us
    pallas_call x1, Pallas kernels, local(): pl.pallas_call(attend_kernel, out_shape=pltpu.VMEM((members, pair, rows,...  0.71 us
    pallas_call x1, Pallas kernels, local(): pl.pallas_call(unpack_kernel, out_shape=pltpu.HBM((tiles, members, pair,...  0.67 us
  transfers between devices with their start and end apart: 1, of which 1 were waited for; matrix products, arithmetic and copies ran while one was open for 0% of the time, Pallas kernels for 0%

profile of v1, /device:TPU:0, one launch (start us, length us, event | category | flops | bytes accessed | tf_op | source)
XLA Modules:
  0.0 32.2 jit_solution(2220892011497044629)
XLA Ops:
  0.0 1.1 %shard_map.64 = (bf16[16,3,2,2,8,128]{5,4,3,2,1,0:T(8,128)(2,1)S(1)}, f32[8,128]{1,0:T(8,128)S(1)}) custom-call(s32[2]{0:T(128)} %levels_ref.1, s32[2]{0:T(128)} %ids_ref.1, f32[32,4096]{1,0:T(8,128)} %gate_ref.1, bf16[2,16,2,8,128]{4,3,2,1,0:T(8,128)(2,1)} %bitcast.18, bf16[2,16,2,8,128]{4,3,2,1,0:T(8,128)(2,1)} %bitcast.19, ...), custom_call_target="tpu_custom_call" | custom-call | tf_op jit(solution)/shard_map/pallas_call | solution.py:116
  1.1 17.6 %all_to_all.10.own_ref = bf16[16,96,128]{2,1,0:T(8,128)(2,1)S(1)} all-to-all(bf16[16,96,128]{2,1,0:T(8,128)(2,1)S(1)} %bitcast.17), channel_id=1, replica_groups={{11,3,15,7,9,1,13,5,10,2,14,6,8,0,12,4},{27,19,31,23,25,17,29,21,26,18,..., dimensions={0} | all-to-all | bytes 786432 | tf_op jit(solution)/shard_map/all_to_all | solution.py:104
  18.7 0.0 collective-permute-start
  18.7 1.7 %collective-permute-done.other_ref = bf16[16,96,128]{2,1,0:T(8,128)(2,1)S(1)} collective-permute-done((bf16[16,96,128]{2,1,0:T(8,128)(2,1)S(1)}, bf16[16,96,128]{2,1,0:T(8,128)(2,1)S(1)}, u32[]{:S(2)}, u32[]{:S(2)}) %collective-permute-start) | collective-permute-done | bytes 393248 | tf_op jit(solution)/shard_map/ppermute | solution.py:132
  20.4 0.7 %shard_map.65 = bf16[16,2,16,128]{3,2,1,0:T(8,128)(2,1)S(1)} custom-call(f32[8,128]{1,0:T(8,128)S(1)} %get-tuple-element.7.side_ref, bf16[16,96,128]{2,1,0:T(8,128)(2,1)S(1)} %all_to_all.10.own_ref, bf16[16,96,128]{2,1,0:T(8,128)(2,1)S(1)} %collective-permute-done.other_ref), custom_call_target="tpu_custom_call" | custom-call | tf_op jit(solution)/shard_map/pallas_call | solution.py:133
  21.1 10.5 %all_to_all.11 = bf16[16,32,128]{2,1,0:T(8,128)(2,1)S(1)} all-to-all(bf16[16,32,128]{2,1,0:T(8,128)(2,1)S(1)} %bitcast.15), channel_id=1, replica_groups={{11,3,15,7,9,1,13,5,10,2,14,6,8,0,12,4},{27,19,31,23,25,17,29,21,26,18,..., dimensions={0} | all-to-all | bytes 262144 | tf_op jit(solution)/shard_map/all_to_all | solution.py:104
  31.6 0.7 %shard_map.66 = bf16[2,16,2,8,128]{4,3,2,1,0:T(8,128)(2,1)} custom-call(bf16[16,2,2,8,128]{4,3,2,1,0:T(8,128)(2,1)S(1)} %bitcast.16), custom_call_target="tpu_custom_call" | custom-call | tf_op jit(solution)/shard_map/pallas_call | solution.py:140
Async XLA Ops:
  18.7 1.7 %collective-permute-start = (bf16[16,96,128]{2,1,0:T(8,128)(2,1)S(1)}, bf16[16,96,128]{2,1,0:T(8,128)(2,1)S(1)}, u32[]{:S(2)}, u32[]{:S(2)}) collective-permute-start(bf16[16,96,128]{2,1,0:T(8,128)(2,1)S(1)} %all_to_all.10.own_ref), channel_id=1, source_target_pairs={{0,16},{16,0},{1,17},{17,1},{2,18},{18,2},{3,19},{19,3},{4,20},{20... | collective-permute-start | bytes 1179656 | tf_op jit(solution)/shard_map/ppermute | solution.py:132

commit v2 on v1

--- a/solution.py
+++ b/solution.py
@@ -1,3 +1,5 @@
+import functools
+
 import jax
 import jax.numpy as jnp
 from jax import lax
@@ -10,19 +12,19 @@
 LOG2_E = 1.4426950408889634
 TILE = 8
 FIRST = 11
-BITS = (3, 2, 1, 0)
-
-
-def member_at(place):
-    return FIRST ^ sum((place >> bit & 1) << to for bit, to in enumerate(BITS))
-
-
-def place_of(member):
-    return sum(((member ^ FIRST) >> to & 1) << bit for bit, to in enumerate(BITS))
-
-
-def members_by_place(members):
-    return [[member_at(place) for place in range(members)]]
+SWAPPED = (0,)
+
+
+def teams(members):
+    order = [place ^ FIRST for place in range(members)]
+    return [[(team ^ (member in SWAPPED)) * members + member for member in order] for team in range(2)]
+
+
+def own_team():
+    team = lax.axis_index("group")
+    for member in SWAPPED:
+        team = jnp.where(lax.axis_index("ctx") == member, 1 - team, team)
+    return team
 
 
 def pack_kernel(
@@ -30,7 +32,7 @@
     packed_ref, side_ref, levels, ids, gate_block, sems,
 ):
     width = gate_block.shape[1]
-    place = place_of(lax.axis_index("ctx"))
+    place = lax.axis_index("ctx") ^ FIRST
     columns = pl.ds(pl.multiple_of(place * width, width), width)
     pairs = [(levels_ref, levels), (ids_ref, ids), (gate_ref.at[:, columns], gate_block)]
     for part, ref in enumerate((query_ref, key_ref, value_ref)):
@@ -41,13 +43,25 @@
         fetch.start()
     for fetch in fetches[:3]:
         fetch.wait()
-    own = lax.axis_index("group")
+    own = own_team()
     other = 1 - own
     level_rows = lax.broadcasted_iota(jnp.int32, gate_block.shape, 0)
-    gate = jnp.sum(jnp.where(level_rows == levels[other], gate_block[...], 0.0), axis=0, keepdims=True)
-    mask = jnp.full((1, HEAD), jnp.where(ids[own] <= ids[other], 0.0, -1e30), jnp.float32)
-    parts = [gate[:, at : at + HEAD] for at in range(0, width, HEAD)]
-    side_ref[pl.ds(0, len(parts) + 1), :] = jnp.concatenate([*parts, mask], axis=0)
+
+    def gate(group):
+        return jnp.sum(jnp.where(level_rows == levels[group], gate_block[...], 0.0), axis=0, keepdims=True)
+
+    keys = side_ref.shape[1]
+    key_place = lax.broadcasted_iota(jnp.int32, (1, keys), 1) // (keys // packed_ref.shape[0])
+    key_swapped = functools.reduce(jnp.logical_or, [key_place == member ^ FIRST for member in SWAPPED])
+    straight = jnp.where(ids[own] <= ids[other], 0.0, -1e30)
+    crossed = jnp.where(ids[other] <= ids[own], 0.0, -1e30)
+    masks = [
+        jnp.where(key_swapped, 0.0, straight),
+        jnp.where(key_swapped, straight, 0.0),
+        jnp.where(key_swapped, crossed, 0.0),
+        jnp.where(key_swapped, 0.0, crossed),
+    ]
+    side_ref[pl.ds(0, 6), :] = jnp.concatenate([gate(other), gate(own), *masks], axis=0)
     for fetch in fetches[3:]:
         fetch.wait()
 
@@ -56,6 +70,9 @@
     members, pair, rows, _ = out_ref.shape
     group_rows = members * rows
     factor = LOG2_E / HEAD**0.5
+    swapped = [place ^ FIRST in SWAPPED for place in range(members)]
+    cuts = [0, *(place for place in range(1, members) if swapped[place] != swapped[place - 1]), members]
+    runs = [(slice(start * rows, stop * rows), swapped[start]) for start, stop in zip(cuts, cuts[1:])]
 
     def tokens(ref, part, head):
         return ref[:, pl.ds((part * pair + head) * rows, rows), :].reshape(group_rows, HEAD)
@@ -63,18 +80,22 @@
     def dot(a, b, contract):
         return lax.dot_general(a, b, ((contract[:1], contract[1:]), ((), ())), preferred_element_type=jnp.float32)
 
+    def masked(score, side):
+        masks = [side_ref[2 + 2 * kind + side : 3 + 2 * kind + side, :] for kind in range(2)]
+        return jnp.concatenate([score[run] + masks[kind] for run, kind in runs], axis=0)
+
     ones = jnp.ones((group_rows, HEAD), jnp.bfloat16)
-    mask = jnp.concatenate([side_ref[pair : pair + 1, :]] * (group_rows // HEAD), axis=1)
     for head in range(pair):
         queries = tokens(other_ref, 0, head)
-        scores = [dot(queries, tokens(ref, 1, head), (1, 1)) for ref in (own_ref, other_ref)]
-        scores[0] = scores[0] + mask
+        refs = (own_ref, other_ref)
+        scores = [masked(dot(queries, tokens(ref, 1, head), (1, 1)), side) for side, ref in enumerate(refs)]
         peak = jnp.max(jnp.maximum(*scores), axis=1, keepdims=True)
         weights = [jnp.exp2((score - peak) * factor).astype(jnp.bfloat16) for score in scores]
-        values = [jnp.concatenate([tokens(ref, 2, head), ones], axis=1) for ref in (own_ref, other_ref)]
+        values = [jnp.concatenate([tokens(ref, 2, head), ones], axis=1) for ref in refs]
         summed = sum(dot(weight, value, (1, 0)) for weight, value in zip(weights, values))
-        attended = (summed[:, :HEAD] / summed[:, HEAD:]).astype(jnp.bfloat16)
-        done = (attended.astype(jnp.float32) * side_ref[head : head + 1, :]).astype(jnp.bfloat16)
+        attended = (summed[:, :HEAD] / summed[:, HEAD:]).astype(jnp.bfloat16).astype(jnp.float32)
+        gates = [side_ref[kind : kind + 1, head * HEAD : (head + 1) * HEAD] for kind in range(2)]
+        done = jnp.concatenate([attended[run] * gates[kind] for run, kind in runs], axis=0).astype(jnp.bfloat16)
         out_ref[:, head] = done.reshape(members, rows, HEAD)
 
 
@@ -100,8 +121,8 @@
 
 
 def exchanged(chunks):
-    members = members_by_place(chunks.shape[0])
-    return lax.all_to_all(chunks, "ctx", split_axis=0, concat_axis=0, tiled=True, axis_index_groups=members)
+    groups = teams(chunks.shape[0])
+    return lax.all_to_all(chunks, ("group", "ctx"), split_axis=0, concat_axis=0, tiled=True, axis_index_groups=groups)
 
 
 def local(queries, key_states, value_states, gate_table, noise_levels, group_ids):
@@ -117,7 +138,7 @@
         pack_kernel,
         out_shape=[
             pltpu.VMEM((members, 3, pair, tiles, TILE, HEAD), jnp.bfloat16),
-            pltpu.VMEM((8, HEAD), jnp.float32),
+            pltpu.VMEM((8, members * rows), jnp.float32),
         ],
         in_specs=[hbm] * len(sources),
         out_specs=[whole, whole],
@@ -228,7 +249,7 @@
 
 
 def solution(mesh):
-    in_pairs = mesh.shape["group"] == 2 and 2 * mesh.shape["ctx"] == HEADS == 2 << len(BITS)
+    in_pairs = mesh.shape["group"] == 2 and 2 * mesh.shape["ctx"] == HEADS
     tokens = P(("group", "ctx"), None)
     return jax.shard_map(
         local if in_pairs else local_wide,

time: 32.5 us -> 31.5 us (0.969)
  the two profiles are of different devices: /device:TPU:0 before, /device:TPU:1 now
where the time goes in v2:
time: 31.5 us; the launch traced here: 31.3 us
  blocking collectives  27.1 us (86%)
  Pallas kernels  2.47 us (8%)
  waiting for transfers between devices  1.72 us (5%)
    all_to_all x2, blocking collectives, exchanged(): lax.all_to_all(chunks, ('group', 'ctx'), split_axis=0, concat_axis=0, til...  27.1 us
    ppermute x1, waiting for transfers between devices, local(): other = lax.ppermute(own, 'group', [(0, 1), (1, 0)])  1.72 us
    pallas_call x1, Pallas kernels, local(): pl.pallas_call(pack_kernel, out_shape=[pltpu.VMEM((members, 3, pair, tile...  1.09 us
    pallas_call x1, Pallas kernels, local(): pl.pallas_call(attend_kernel, out_shape=pltpu.VMEM((members, pair, rows,...  0.71 us
    pallas_call x1, Pallas kernels, local(): pl.pallas_call(unpack_kernel, out_shape=pltpu.HBM((tiles, members, pair,...  0.67 us
  transfers between devices with their start and end apart: 1, of which 1 were waited for; matrix products, arithmetic and copies ran while one was open for 0% of the time, Pallas kernels for 0%

profile of v2, /device:TPU:1, one launch (start us, length us, event | category | flops | bytes accessed | tf_op | source)
XLA Modules:
  0.0 31.3 jit_solution(3288285903325403822)
XLA Ops:
  0.0 1.1 %shard_map.64 = (bf16[16,3,2,2,8,128]{5,4,3,2,1,0:T(8,128)(2,1)S(1)}, f32[8,256]{1,0:T(8,128)S(1)}) custom-call(s32[2]{0:T(128)} %levels_ref.1, s32[2]{0:T(128)} %ids_ref.1, f32[32,4096]{1,0:T(8,128)} %gate_ref.1, bf16[2,16,2,8,128]{4,3,2,1,0:T(8,128)(2,1)} %bitcast.18, bf16[2,16,2,8,128]{4,3,2,1,0:T(8,128)(2,1)} %bitcast.19, ...), custom_call_target="tpu_custom_call" | custom-call | tf_op jit(solution)/shard_map/pallas_call | solution.py:137
  1.1 16.8 %all_to_all.10.own_ref = bf16[16,96,128]{2,1,0:T(8,128)(2,1)S(1)} all-to-all(bf16[16,96,128]{2,1,0:T(8,128)(2,1)S(1)} %bitcast.17), channel_id=1, replica_groups={{11,10,9,8,15,14,13,12,3,2,1,16,7,6,5,4},{27,26,25,24,31,30,29,28,19,18..., dimensions={0} | all-to-all | bytes 786432 | tf_op jit(solution)/shard_map/all_to_all | solution.py:125
  17.9 0.0 collective-permute-start
  17.9 1.7 %collective-permute-done.other_ref = bf16[16,96,128]{2,1,0:T(8,128)(2,1)S(1)} collective-permute-done((bf16[16,96,128]{2,1,0:T(8,128)(2,1)S(1)}, bf16[16,96,128]{2,1,0:T(8,128)(2,1)S(1)}, u32[]{:S(2)}, u32[]{:S(2)}) %collective-permute-start) | collective-permute-done | bytes 393248 | tf_op jit(solution)/shard_map/ppermute | solution.py:153
  19.7 0.7 %shard_map.65 = bf16[16,2,16,128]{3,2,1,0:T(8,128)(2,1)S(1)} custom-call(f32[8,256]{1,0:T(8,128)S(1)} %get-tuple-element.7.side_ref, bf16[16,96,128]{2,1,0:T(8,128)(2,1)S(1)} %all_to_all.10.own_ref, bf16[16,96,128]{2,1,0:T(8,128)(2,1)S(1)} %collective-permute-done.other_ref), custom_call_target="tpu_custom_call" | custom-call | tf_op jit(solution)/shard_map/pallas_call | solution.py:154
  20.4 10.3 %all_to_all.11 = bf16[16,32,128]{2,1,0:T(8,128)(2,1)S(1)} all-to-all(bf16[16,32,128]{2,1,0:T(8,128)(2,1)S(1)} %bitcast.15), channel_id=1, replica_groups={{11,10,9,8,15,14,13,12,3,2,1,16,7,6,5,4},{27,26,25,24,31,30,29,28,19,18..., dimensions={0} | all-to-all | bytes 262144 | tf_op jit(solution)/shard_map/all_to_all | solution.py:125
  30.6 0.7 %shard_map.66 = bf16[2,16,2,8,128]{4,3,2,1,0:T(8,128)(2,1)} custom-call(bf16[16,2,2,8,128]{4,3,2,1,0:T(8,128)(2,1)S(1)} %bitcast.16), custom_call_target="tpu_custom_call" | custom-call | tf_op jit(solution)/shard_map/pallas_call | solution.py:161
Async XLA Ops:
  17.9 1.7 %collective-permute-start = (bf16[16,96,128]{2,1,0:T(8,128)(2,1)S(1)}, bf16[16,96,128]{2,1,0:T(8,128)(2,1)S(1)}, u32[]{:S(2)}, u32[]{:S(2)}) collective-permute-start(bf16[16,96,128]{2,1,0:T(8,128)(2,1)S(1)} %all_to_all.10.own_ref), channel_id=1, source_target_pairs={{0,16},{16,0},{1,17},{17,1},{2,18},{18,2},{3,19},{19,3},{4,20},{20... | collective-permute-start | bytes 1179656 | tf_op jit(solution)/shard_map/ppermute | solution.py:153

commit v3 on v2

--- a/solution.py
+++ b/solution.py
@@ -13,10 +13,24 @@
 TILE = 8
 FIRST = 11
 SWAPPED = (0,)
-
-
-def teams(members):
-    order = [place ^ FIRST for place in range(members)]
+STATES_BITS = (3, 2, 1, 0)
+DONE_BITS = (0, 1, 2, 3)
+
+
+def member_at(place, bits):
+    return FIRST ^ sum((place >> bit & 1) << to for bit, to in enumerate(bits))
+
+
+def place_of(member, bits):
+    return sum(((member ^ FIRST) >> to & 1) << bit for bit, to in enumerate(bits))
+
+
+def done_place(place):
+    return place_of(member_at(place, STATES_BITS), DONE_BITS)
+
+
+def teams(members, bits):
+    order = [member_at(place, bits) for place in range(members)]
     return [[(team ^ (member in SWAPPED)) * members + member for member in order] for team in range(2)]
 
 
@@ -32,7 +46,7 @@
     packed_ref, side_ref, levels, ids, gate_block, sems,
 ):
     width = gate_block.shape[1]
-    place = lax.axis_index("ctx") ^ FIRST
+    place = place_of(lax.axis_index("ctx"), STATES_BITS)
     columns = pl.ds(pl.multiple_of(place * width, width), width)
     pairs = [(levels_ref, levels), (ids_ref, ids), (gate_ref.at[:, columns], gate_block)]
     for part, ref in enumerate((query_ref, key_ref, value_ref)):
@@ -52,7 +66,7 @@
 
     keys = side_ref.shape[1]
     key_place = lax.broadcasted_iota(jnp.int32, (1, keys), 1) // (keys // packed_ref.shape[0])
-    key_swapped = functools.reduce(jnp.logical_or, [key_place == member ^ FIRST for member in SWAPPED])
+    key_swapped = functools.reduce(jnp.logical_or, [key_place == place_of(member, STATES_BITS) for member in SWAPPED])
     straight = jnp.where(ids[own] <= ids[other], 0.0, -1e30)
     crossed = jnp.where(ids[other] <= ids[own], 0.0, -1e30)
     masks = [
@@ -70,7 +84,7 @@
     members, pair, rows, _ = out_ref.shape
     group_rows = members * rows
     factor = LOG2_E / HEAD**0.5
-    swapped = [place ^ FIRST in SWAPPED for place in range(members)]
+    swapped = [member_at(place, STATES_BITS) in SWAPPED for place in range(members)]
     cuts = [0, *(place for place in range(1, members) if swapped[place] != swapped[place - 1]), members]
     runs = [(slice(start * rows, stop * rows), swapped[start]) for start, stop in zip(cuts, cuts[1:])]
 
@@ -96,18 +110,15 @@
         attended = (summed[:, :HEAD] / summed[:, HEAD:]).astype(jnp.bfloat16).astype(jnp.float32)
         gates = [side_ref[kind : kind + 1, head * HEAD : (head + 1) * HEAD] for kind in range(2)]
         done = jnp.concatenate([attended[run] * gates[kind] for run, kind in runs], axis=0).astype(jnp.bfloat16)
-        out_ref[:, head] = done.reshape(members, rows, HEAD)
-
-
-def unpack_kernel(heads_ref, out_ref, sems):
-    copies = [
-        pltpu.make_async_copy(heads_ref.at[:, :, tile], out_ref.at[tile], sems.at[tile])
-        for tile in range(out_ref.shape[0])
-    ]
-    for copy in copies:
-        copy.start()
-    for copy in copies:
-        copy.wait()
+        for place in range(members):
+            out_ref[done_place(place), head] = done[place * rows : (place + 1) * rows]
+
+
+def unpack_kernel(heads_ref, out_ref):
+    members, pair, rows, _ = heads_ref.shape
+    for place in range(members):
+        for head in range(pair):
+            out_ref[:, pl.ds((place * pair + head) * HEAD, HEAD)] = heads_ref[done_place(place), head]
 
 
 def in_vmem(array):
@@ -120,8 +131,8 @@
     return states.reshape(rows // TILE, TILE, members, pair, HEAD).transpose(0, 2, 3, 1, 4)
 
 
-def exchanged(chunks):
-    groups = teams(chunks.shape[0])
+def exchanged(chunks, bits):
+    groups = teams(chunks.shape[0], bits)
     return lax.all_to_all(chunks, ("group", "ctx"), split_axis=0, concat_axis=0, tiled=True, axis_index_groups=groups)
 
 
@@ -149,7 +160,7 @@
             pltpu.SemaphoreType.DMA((3 + 3 * tiles,)),
         ],
     )(*(pltpu.with_memory_space_constraint(source, pltpu.HBM) for source in sources))
-    own = exchanged(packed.reshape(members, 3 * pair * rows, HEAD))
+    own = exchanged(packed.reshape(members, 3 * pair * rows, HEAD), STATES_BITS)
     other = lax.ppermute(own, "group", [(0, 1), (1, 0)])
     done = pl.pallas_call(
         attend_kernel,
@@ -157,15 +168,13 @@
         in_specs=[whole] * 3,
         out_specs=whole,
     )(in_vmem(side), in_vmem(own), in_vmem(other))
-    returned = exchanged(done.reshape(members, pair * rows, HEAD))
-    handed = pl.pallas_call(
+    returned = exchanged(done.reshape(members, pair * rows, HEAD), DONE_BITS)
+    return pl.pallas_call(
         unpack_kernel,
-        out_shape=pltpu.HBM((tiles, members, pair, TILE, HEAD), jnp.bfloat16),
+        out_shape=jax.ShapeDtypeStruct((rows, HEADS * HEAD), jnp.bfloat16),
         in_specs=[whole],
-        out_specs=hbm,
-        scratch_shapes=[pltpu.SemaphoreType.DMA((tiles,))],
-    )(in_vmem(returned.reshape(members, pair, tiles, TILE, HEAD)))
-    return handed.transpose(0, 3, 1, 2, 4).reshape(rows, HEADS * HEAD)
+        out_specs=whole,
+    )(in_vmem(returned.reshape(members, pair, rows, HEAD)))
 
 
 def shifted(block, axis, distance):
@@ -249,7 +258,7 @@
 
 
 def solution(mesh):
-    in_pairs = mesh.shape["group"] == 2 and 2 * mesh.shape["ctx"] == HEADS
+    in_pairs = mesh.shape["group"] == 2 and 2 * mesh.shape["ctx"] == HEADS == 2 << len(STATES_BITS)
     tokens = P(("group", "ctx"), None)
     return jax.shard_map(
         local if in_pairs else local_wide,

time: 31.5 us -> 31.6 us (level)
  no operation moved by 1% of the time
where the time goes in v3:
time: 31.6 us; the launch traced here: 31.3 us
  blocking collectives  27.1 us (86%)
  Pallas kernels  2.48 us (8%)
  waiting for transfers between devices  1.72 us (5%)
    all_to_all x2, blocking collectives, exchanged(): lax.all_to_all(chunks, ('group', 'ctx'), split_axis=0, concat_axis=0, til...  27.1 us
    ppermute x1, waiting for transfers between devices, local(): other = lax.ppermute(own, 'group', [(0, 1), (1, 0)])  1.72 us
    pallas_call x1, Pallas kernels, local(): pl.pallas_call(pack_kernel, out_shape=[pltpu.VMEM((members, 3, pair, tile...  1.09 us
    pallas_call x1, Pallas kernels, local(): pl.pallas_call(attend_kernel, out_shape=pltpu.VMEM((members, pair, rows,...  0.71 us
    pallas_call x1, Pallas kernels, local(): pl.pallas_call(unpack_kernel, out_shape=jax.ShapeDtypeStruct((rows, HEADS...  0.68 us
  transfers between devices with their start and end apart: 1, of which 1 were waited for; matrix products, arithmetic and copies ran while one was open for 0% of the time, Pallas kernels for 0%

profile of v3, /device:TPU:1, one launch (start us, length us, event | category | flops | bytes accessed | tf_op | source)
XLA Modules:
  0.0 31.3 jit_solution(3080225587330215613)
XLA Ops:
  0.0 1.1 %shard_map.64 = (bf16[16,3,2,2,8,128]{5,4,3,2,1,0:T(8,128)(2,1)S(1)}, f32[8,256]{1,0:T(8,128)S(1)}) custom-call(s32[2]{0:T(128)} %levels_ref.1, s32[2]{0:T(128)} %ids_ref.1, f32[32,4096]{1,0:T(8,128)} %gate_ref.1, bf16[2,16,2,8,128]{4,3,2,1,0:T(8,128)(2,1)} %bitcast.15, bf16[2,16,2,8,128]{4,3,2,1,0:T(8,128)(2,1)} %bitcast.16, ...), custom_call_target="tpu_custom_call" | custom-call | tf_op jit(solution)/shard_map/pallas_call | solution.py:148
  1.1 16.9 %all_to_all.10.own_ref = bf16[16,96,128]{2,1,0:T(8,128)(2,1)S(1)} all-to-all(bf16[16,96,128]{2,1,0:T(8,128)(2,1)S(1)} %bitcast.14), channel_id=1, replica_groups={{11,3,15,7,9,1,13,5,10,2,14,6,8,16,12,4},{27,19,31,23,25,17,29,21,26,18..., dimensions={0} | all-to-all | bytes 786432 | tf_op jit(solution)/shard_map/all_to_all | solution.py:136
  18.0 0.0 collective-permute-start
  18.0 1.7 %collective-permute-done.other_ref = bf16[16,96,128]{2,1,0:T(8,128)(2,1)S(1)} collective-permute-done((bf16[16,96,128]{2,1,0:T(8,128)(2,1)S(1)}, bf16[16,96,128]{2,1,0:T(8,128)(2,1)S(1)}, u32[]{:S(2)}, u32[]{:S(2)}) %collective-permute-start) | collective-permute-done | bytes 393248 | tf_op jit(solution)/shard_map/ppermute | solution.py:164
  19.8 0.7 %shard_map.65 = bf16[16,2,16,128]{3,2,1,0:T(8,128)(2,1)S(1)} custom-call(f32[8,256]{1,0:T(8,128)S(1)} %get-tuple-element.7.side_ref, bf16[16,96,128]{2,1,0:T(8,128)(2,1)S(1)} %all_to_all.10.own_ref, bf16[16,96,128]{2,1,0:T(8,128)(2,1)S(1)} %collective-permute-done.other_ref), custom_call_target="tpu_custom_call" | custom-call | tf_op jit(solution)/shard_map/pallas_call | solution.py:165
  20.5 10.2 %all_to_all.11 = bf16[16,32,128]{2,1,0:T(8,128)(2,1)S(1)} all-to-all(bf16[16,32,128]{2,1,0:T(8,128)(2,1)S(1)} %bitcast.12), channel_id=1, replica_groups={{11,10,9,8,15,14,13,12,3,2,1,16,7,6,5,4},{27,26,25,24,31,30,29,28,19,18..., dimensions={0} | all-to-all | bytes 262144 | tf_op jit(solution)/shard_map/all_to_all | solution.py:136
  30.7 0.7 %shard_map.66 = bf16[16,4096]{1,0:T(8,128)(2,1)} custom-call(bf16[16,2,16,128]{3,2,1,0:T(8,128)(2,1)S(1)} %bitcast.13), custom_call_target="tpu_custom_call" | custom-call | tf_op jit(solution)/shard_map/pallas_call | solution.py:172
Async XLA Ops:
  18.0 1.7 %collective-permute-start = (bf16[16,96,128]{2,1,0:T(8,128)(2,1)S(1)}, bf16[16,96,128]{2,1,0:T(8,128)(2,1)S(1)}, u32[]{:S(2)}, u32[]{:S(2)}) collective-permute-start(bf16[16,96,128]{2,1,0:T(8,128)(2,1)S(1)} %all_to_all.10.own_ref), channel_id=1, source_target_pairs={{0,16},{16,0},{1,17},{17,1},{2,18},{18,2},{3,19},{19,3},{4,20},{20... | collective-permute-start | bytes 1179656 | tf_op jit(solution)/shard_map/ppermute | solution.py:164

commit v4 on v2

--- a/solution.py
+++ b/solution.py
@@ -12,11 +12,20 @@
 LOG2_E = 1.4426950408889634
 TILE = 8
 FIRST = 11
+STEP = -1
 SWAPPED = (0,)
 
 
+def member_at(place, members):
+    return (FIRST + STEP * place) % members
+
+
+def place_of(member, members):
+    return (member - FIRST) * STEP % members
+
+
 def teams(members):
-    order = [place ^ FIRST for place in range(members)]
+    order = [member_at(place, members) for place in range(members)]
     return [[(team ^ (member in SWAPPED)) * members + member for member in order] for team in range(2)]
 
 
@@ -32,7 +41,8 @@
     packed_ref, side_ref, levels, ids, gate_block, sems,
 ):
     width = gate_block.shape[1]
-    place = lax.axis_index("ctx") ^ FIRST
+    members = packed_ref.shape[0]
+    place = (FIRST + members - lax.axis_index("ctx")) % members
     columns = pl.ds(pl.multiple_of(place * width, width), width)
     pairs = [(levels_ref, levels), (ids_ref, ids), (gate_ref.at[:, columns], gate_block)]
     for part, ref in enumerate((query_ref, key_ref, value_ref)):
@@ -52,7 +62,7 @@
 
     keys = side_ref.shape[1]
     key_place = lax.broadcasted_iota(jnp.int32, (1, keys), 1) // (keys // packed_ref.shape[0])
-    key_swapped = functools.reduce(jnp.logical_or, [key_place == member ^ FIRST for member in SWAPPED])
+    key_swapped = functools.reduce(jnp.logical_or, [key_place == place_of(member, members) for member in SWAPPED])
     straight = jnp.where(ids[own] <= ids[other], 0.0, -1e30)
     crossed = jnp.where(ids[other] <= ids[own], 0.0, -1e30)
     masks = [
@@ -70,7 +80,7 @@
     members, pair, rows, _ = out_ref.shape
     group_rows = members * rows
     factor = LOG2_E / HEAD**0.5
-    swapped = [place ^ FIRST in SWAPPED for place in range(members)]
+    swapped = [member_at(place, members) in SWAPPED for place in range(members)]
     cuts = [0, *(place for place in range(1, members) if swapped[place] != swapped[place - 1]), members]
     runs = [(slice(start * rows, stop * rows), swapped[start]) for start, stop in zip(cuts, cuts[1:])]
 

time: 31.5 us -> 31.8 us (level)
  no operation moved by 1% of the time
where the time goes in v4:
time: 31.8 us; the launch traced here: 31.6 us
  blocking collectives  27.4 us (86%)
  Pallas kernels  2.47 us (8%)
  waiting for transfers between devices  1.72 us (5%)
    all_to_all x2, blocking collectives, exchanged(): lax.all_to_all(chunks, ('group', 'ctx'), split_axis=0, concat_axis=0, til...  27.4 us
    ppermute x1, waiting for transfers between devices, local(): other = lax.ppermute(own, 'group', [(0, 1), (1, 0)])  1.72 us
    pallas_call x1, Pallas kernels, local(): pl.pallas_call(pack_kernel, out_shape=[pltpu.VMEM((members, 3, pair, tile...  1.09 us
    pallas_call x1, Pallas kernels, local(): pl.pallas_call(attend_kernel, out_shape=pltpu.VMEM((members, pair, rows,...  0.71 us
    pallas_call x1, Pallas kernels, local(): pl.pallas_call(unpack_kernel, out_shape=pltpu.HBM((tiles, members, pair,...  0.67 us
  transfers between devices with their start and end apart: 1, of which 1 were waited for; matrix products, arithmetic and copies ran while one was open for 0% of the time, Pallas kernels for 0%

profile of v4, /device:TPU:1, one launch (start us, length us, event | category | flops | bytes accessed | tf_op | source)
XLA Modules:
  0.0 31.6 jit_solution(1187286731384454633)
XLA Ops:
  0.0 1.1 %shard_map.64 = (bf16[16,3,2,2,8,128]{5,4,3,2,1,0:T(8,128)(2,1)S(1)}, f32[8,256]{1,0:T(8,128)S(1)}) custom-call(s32[2]{0:T(128)} %levels_ref.1, s32[2]{0:T(128)} %ids_ref.1, f32[32,4096]{1,0:T(8,128)} %gate_ref.1, bf16[2,16,2,8,128]{4,3,2,1,0:T(8,128)(2,1)} %bitcast.18, bf16[2,16,2,8,128]{4,3,2,1,0:T(8,128)(2,1)} %bitcast.19, ...), custom_call_target="tpu_custom_call" | custom-call | tf_op jit(solution)/shard_map/pallas_call | solution.py:147
  1.1 17.1 %all_to_all.10.own_ref = bf16[16,96,128]{2,1,0:T(8,128)(2,1)S(1)} all-to-all(bf16[16,96,128]{2,1,0:T(8,128)(2,1)S(1)} %bitcast.17), channel_id=1, replica_groups={{11,10,9,8,7,6,5,4,3,2,1,16,15,14,13,12},{27,26,25,24,23,22,21,20,19,18..., dimensions={0} | all-to-all | bytes 786432 | tf_op jit(solution)/shard_map/all_to_all | solution.py:135
  18.2 0.0 collective-permute-start
  18.2 1.7 %collective-permute-done.other_ref = bf16[16,96,128]{2,1,0:T(8,128)(2,1)S(1)} collective-permute-done((bf16[16,96,128]{2,1,0:T(8,128)(2,1)S(1)}, bf16[16,96,128]{2,1,0:T(8,128)(2,1)S(1)}, u32[]{:S(2)}, u32[]{:S(2)}) %collective-permute-start) | collective-permute-done | bytes 393248 | tf_op jit(solution)/shard_map/ppermute | solution.py:163
  20.0 0.7 %shard_map.65 = bf16[16,2,16,128]{3,2,1,0:T(8,128)(2,1)S(1)} custom-call(f32[8,256]{1,0:T(8,128)S(1)} %get-tuple-element.7.side_ref, bf16[16,96,128]{2,1,0:T(8,128)(2,1)S(1)} %all_to_all.10.own_ref, bf16[16,96,128]{2,1,0:T(8,128)(2,1)S(1)} %collective-permute-done.other_ref), custom_call_target="tpu_custom_call" | custom-call | tf_op jit(solution)/shard_map/pallas_call | solution.py:164
  20.7 10.2 %all_to_all.11 = bf16[16,32,128]{2,1,0:T(8,128)(2,1)S(1)} all-to-all(bf16[16,32,128]{2,1,0:T(8,128)(2,1)S(1)} %bitcast.15), channel_id=1, replica_groups={{11,10,9,8,7,6,5,4,3,2,1,16,15,14,13,12},{27,26,25,24,23,22,21,20,19,18..., dimensions={0} | all-to-all | bytes 262144 | tf_op jit(solution)/shard_map/all_to_all | solution.py:135
  30.9 0.7 %shard_map.66 = bf16[2,16,2,8,128]{4,3,2,1,0:T(8,128)(2,1)} custom-call(bf16[16,2,2,8,128]{4,3,2,1,0:T(8,128)(2,1)S(1)} %bitcast.16), custom_call_target="tpu_custom_call" | custom-call | tf_op jit(solution)/shard_map/pallas_call | solution.py:171
Async XLA Ops:
  18.2 1.7 %collective-permute-start = (bf16[16,96,128]{2,1,0:T(8,128)(2,1)S(1)}, bf16[16,96,128]{2,1,0:T(8,128)(2,1)S(1)}, u32[]{:S(2)}, u32[]{:S(2)}) collective-permute-start(bf16[16,96,128]{2,1,0:T(8,128)(2,1)S(1)} %all_to_all.10.own_ref), channel_id=1, source_target_pairs={{0,16},{16,0},{1,17},{17,1},{2,18},{18,2},{3,19},{19,3},{4,20},{20... | collective-permute-start | bytes 1179656 | tf_op jit(solution)/shard_map/ppermute | solution.py:163

commit v5 on v2

--- a/solution.py
+++ b/solution.py
@@ -34,14 +34,16 @@
     width = gate_block.shape[1]
     place = lax.axis_index("ctx") ^ FIRST
     columns = pl.ds(pl.multiple_of(place * width, width), width)
-    pairs = [(levels_ref, levels), (ids_ref, ids), (gate_ref.at[:, columns], gate_block)]
+    pairs = []
     for part, ref in enumerate((query_ref, key_ref, value_ref)):
         for tile in range(ref.shape[0]):
             pairs.append((ref.at[tile], packed_ref.at[:, part, :, tile]))
+    count = len(pairs)
+    pairs += [(levels_ref, levels), (ids_ref, ids), (gate_ref.at[:, columns], gate_block)]
     fetches = [pltpu.make_async_copy(*pair, sems.at[i]) for i, pair in enumerate(pairs)]
     for fetch in fetches:
         fetch.start()
-    for fetch in fetches[:3]:
+    for fetch in fetches[count:]:
         fetch.wait()
     own = own_team()
     other = 1 - own
@@ -62,7 +64,7 @@
         jnp.where(key_swapped, 0.0, crossed),
     ]
     side_ref[pl.ds(0, 6), :] = jnp.concatenate([gate(other), gate(own), *masks], axis=0)
-    for fetch in fetches[3:]:
+    for fetch in fetches[:count]:
         fetch.wait()
 
 

time: 31.5 us -> 31.5 us (level)
  no operation moved by 1% of the time
where the time goes in v5:
time: 31.5 us; the launch traced here: 31.3 us
  blocking collectives  27.1 us (86%)
  Pallas kernels  2.45 us (8%)
  waiting for transfers between devices  1.72 us (5%)
    all_to_all x2, blocking collectives, exchanged(): lax.all_to_all(chunks, ('group', 'ctx'), split_axis=0, concat_axis=0, til...  27.1 us
    ppermute x1, waiting for transfers between devices, local(): other = lax.ppermute(own, 'group', [(0, 1), (1, 0)])  1.72 us
    pallas_call x1, Pallas kernels, local(): pl.pallas_call(pack_kernel, out_shape=[pltpu.VMEM((members, 3, pair, tile...  1.07 us
    pallas_call x1, Pallas kernels, local(): pl.pallas_call(attend_kernel, out_shape=pltpu.VMEM((members, pair, rows,...  0.71 us
    pallas_call x1, Pallas kernels, local(): pl.pallas_call(unpack_kernel, out_shape=pltpu.HBM((tiles, members, pair,...  0.67 us
  transfers between devices with their start and end apart: 1, of which 1 were waited for; matrix products, arithmetic and copies ran while one was open for 0% of the time, Pallas kernels for 0%

profile of v5, /device:TPU:1, one launch (start us, length us, event | category | flops | bytes accessed | tf_op | source)
XLA Modules:
  0.0 31.3 jit_solution(11993559700091073971)
XLA Ops:
  0.0 1.1 %shard_map.64 = (bf16[16,3,2,2,8,128]{5,4,3,2,1,0:T(8,128)(2,1)S(1)}, f32[8,256]{1,0:T(8,128)S(1)}) custom-call(s32[2]{0:T(128)} %levels_ref.1, s32[2]{0:T(128)} %ids_ref.1, f32[32,4096]{1,0:T(8,128)} %gate_ref.1, bf16[2,16,2,8,128]{4,3,2,1,0:T(8,128)(2,1)} %bitcast.18, bf16[2,16,2,8,128]{4,3,2,1,0:T(8,128)(2,1)} %bitcast.19, ...), custom_call_target="tpu_custom_call" | custom-call | tf_op jit(solution)/shard_map/pallas_call | solution.py:139
  1.1 16.8 %all_to_all.10.own_ref = bf16[16,96,128]{2,1,0:T(8,128)(2,1)S(1)} all-to-all(bf16[16,96,128]{2,1,0:T(8,128)(2,1)S(1)} %bitcast.17), channel_id=1, replica_groups={{11,10,9,8,15,14,13,12,3,2,1,16,7,6,5,4},{27,26,25,24,31,30,29,28,19,18..., dimensions={0} | all-to-all | bytes 786432 | tf_op jit(solution)/shard_map/all_to_all | solution.py:127
  17.9 0.0 collective-permute-start
  17.9 1.7 %collective-permute-done.other_ref = bf16[16,96,128]{2,1,0:T(8,128)(2,1)S(1)} collective-permute-done((bf16[16,96,128]{2,1,0:T(8,128)(2,1)S(1)}, bf16[16,96,128]{2,1,0:T(8,128)(2,1)S(1)}, u32[]{:S(2)}, u32[]{:S(2)}) %collective-permute-start) | collective-permute-done | bytes 393248 | tf_op jit(solution)/shard_map/ppermute | solution.py:155
  19.6 0.7 %shard_map.65 = bf16[16,2,16,128]{3,2,1,0:T(8,128)(2,1)S(1)} custom-call(f32[8,256]{1,0:T(8,128)S(1)} %get-tuple-element.7.side_ref, bf16[16,96,128]{2,1,0:T(8,128)(2,1)S(1)} %all_to_all.10.own_ref, bf16[16,96,128]{2,1,0:T(8,128)(2,1)S(1)} %collective-permute-done.other_ref), custom_call_target="tpu_custom_call" | custom-call | tf_op jit(solution)/shard_map/pallas_call | solution.py:156
  20.4 10.3 %all_to_all.11 = bf16[16,32,128]{2,1,0:T(8,128)(2,1)S(1)} all-to-all(bf16[16,32,128]{2,1,0:T(8,128)(2,1)S(1)} %bitcast.15), channel_id=1, replica_groups={{11,10,9,8,15,14,13,12,3,2,1,16,7,6,5,4},{27,26,25,24,31,30,29,28,19,18..., dimensions={0} | all-to-all | bytes 262144 | tf_op jit(solution)/shard_map/all_to_all | solution.py:127
  30.6 0.7 %shard_map.66 = bf16[2,16,2,8,128]{4,3,2,1,0:T(8,128)(2,1)} custom-call(bf16[16,2,2,8,128]{4,3,2,1,0:T(8,128)(2,1)S(1)} %bitcast.16), custom_call_target="tpu_custom_call" | custom-call | tf_op jit(solution)/shard_map/pallas_call | solution.py:163
Async XLA Ops:
  17.9 1.7 %collective-permute-start = (bf16[16,96,128]{2,1,0:T(8,128)(2,1)S(1)}, bf16[16,96,128]{2,1,0:T(8,128)(2,1)S(1)}, u32[]{:S(2)}, u32[]{:S(2)}) collective-permute-start(bf16[16,96,128]{2,1,0:T(8,128)(2,1)S(1)} %all_to_all.10.own_ref), channel_id=1, source_target_pairs={{0,16},{16,0},{1,17},{17,1},{2,18},{18,2},{3,19},{19,3},{4,20},{20... | collective-permute-start | bytes 1179656 | tf_op jit(solution)/shard_map/ppermute | solution.py:155

commit v6 on v2

--- a/solution.py
+++ b/solution.py
@@ -85,15 +85,19 @@
         return jnp.concatenate([score[run] + masks[kind] for run, kind in runs], axis=0)
 
     ones = jnp.ones((group_rows, HEAD), jnp.bfloat16)
+    refs = (own_ref, other_ref)
+    scores = [
+        [dot(tokens(other_ref, 0, head), tokens(ref, 1, head), (1, 1)) for ref in refs] for head in range(pair)
+    ]
+    summed = []
     for head in range(pair):
-        queries = tokens(other_ref, 0, head)
-        refs = (own_ref, other_ref)
-        scores = [masked(dot(queries, tokens(ref, 1, head), (1, 1)), side) for side, ref in enumerate(refs)]
-        peak = jnp.max(jnp.maximum(*scores), axis=1, keepdims=True)
-        weights = [jnp.exp2((score - peak) * factor).astype(jnp.bfloat16) for score in scores]
+        blocks = [masked(score, side) for side, score in enumerate(scores[head])]
+        peak = jnp.max(jnp.maximum(*blocks), axis=1, keepdims=True)
+        weights = [jnp.exp2((block - peak) * factor).astype(jnp.bfloat16) for block in blocks]
         values = [jnp.concatenate([tokens(ref, 2, head), ones], axis=1) for ref in refs]
-        summed = sum(dot(weight, value, (1, 0)) for weight, value in zip(weights, values))
-        attended = (summed[:, :HEAD] / summed[:, HEAD:]).astype(jnp.bfloat16).astype(jnp.float32)
+        summed.append(sum(dot(weight, value, (1, 0)) for weight, value in zip(weights, values)))
+    for head in range(pair):
+        attended = (summed[head][:, :HEAD] / summed[head][:, HEAD:]).astype(jnp.bfloat16).astype(jnp.float32)
         gates = [side_ref[kind : kind + 1, head * HEAD : (head + 1) * HEAD] for kind in range(2)]
         done = jnp.concatenate([attended[run] * gates[kind] for run, kind in runs], axis=0).astype(jnp.bfloat16)
         out_ref[:, head] = done.reshape(members, rows, HEAD)

time: 31.5 us -> 31.5 us (level)
  no operation moved by 1% of the time
where the time goes in v6:
time: 31.5 us; the launch traced here: 31.3 us
  blocking collectives  27.1 us (86%)
  Pallas kernels  2.41 us (8%)
  waiting for transfers between devices  1.72 us (5%)
    all_to_all x2, blocking collectives, exchanged(): lax.all_to_all(chunks, ('group', 'ctx'), split_axis=0, concat_axis=0, til...  27.1 us
    ppermute x1, waiting for transfers between devices, local(): other = lax.ppermute(own, 'group', [(0, 1), (1, 0)])  1.72 us
    pallas_call x1, Pallas kernels, local(): pl.pallas_call(pack_kernel, out_shape=[pltpu.VMEM((members, 3, pair, tile...  1.09 us
    pallas_call x1, Pallas kernels, local(): pl.pallas_call(unpack_kernel, out_shape=pltpu.HBM((tiles, members, pair,...  0.67 us
    pallas_call x1, Pallas kernels, local(): pl.pallas_call(attend_kernel, out_shape=pltpu.VMEM((members, pair, rows,...  0.65 us
  transfers between devices with their start and end apart: 1, of which 1 were waited for; matrix products, arithmetic and copies ran while one was open for 0% of the time, Pallas kernels for 0%

profile of v6, /device:TPU:1, one launch (start us, length us, event | category | flops | bytes accessed | tf_op | source)
XLA Modules:
  0.0 31.3 jit_solution(14735288631099855892)
XLA Ops:
  0.0 1.1 %shard_map.64 = (bf16[16,3,2,2,8,128]{5,4,3,2,1,0:T(8,128)(2,1)S(1)}, f32[8,256]{1,0:T(8,128)S(1)}) custom-call(s32[2]{0:T(128)} %levels_ref.1, s32[2]{0:T(128)} %ids_ref.1, f32[32,4096]{1,0:T(8,128)} %gate_ref.1, bf16[2,16,2,8,128]{4,3,2,1,0:T(8,128)(2,1)} %bitcast.18, bf16[2,16,2,8,128]{4,3,2,1,0:T(8,128)(2,1)} %bitcast.19, ...), custom_call_target="tpu_custom_call" | custom-call | tf_op jit(solution)/shard_map/pallas_call | solution.py:141
  1.1 16.8 %all_to_all.10.own_ref = bf16[16,96,128]{2,1,0:T(8,128)(2,1)S(1)} all-to-all(bf16[16,96,128]{2,1,0:T(8,128)(2,1)S(1)} %bitcast.17), channel_id=1, replica_groups={{11,10,9,8,15,14,13,12,3,2,1,16,7,6,5,4},{27,26,25,24,31,30,29,28,19,18..., dimensions={0} | all-to-all | bytes 786432 | tf_op jit(solution)/shard_map/all_to_all | solution.py:129
  17.9 0.0 collective-permute-start
  17.9 1.7 %collective-permute-done.other_ref = bf16[16,96,128]{2,1,0:T(8,128)(2,1)S(1)} collective-permute-done((bf16[16,96,128]{2,1,0:T(8,128)(2,1)S(1)}, bf16[16,96,128]{2,1,0:T(8,128)(2,1)S(1)}, u32[]{:S(2)}, u32[]{:S(2)}) %collective-permute-start) | collective-permute-done | bytes 393248 | tf_op jit(solution)/shard_map/ppermute | solution.py:157
  19.7 0.7 %shard_map.65 = bf16[16,2,16,128]{3,2,1,0:T(8,128)(2,1)S(1)} custom-call(f32[8,256]{1,0:T(8,128)S(1)} %get-tuple-element.7.side_ref, bf16[16,96,128]{2,1,0:T(8,128)(2,1)S(1)} %all_to_all.10.own_ref, bf16[16,96,128]{2,1,0:T(8,128)(2,1)S(1)} %collective-permute-done.other_ref), custom_call_target="tpu_custom_call" | custom-call | tf_op jit(solution)/shard_map/pallas_call | solution.py:158
  20.3 10.3 %all_to_all.11 = bf16[16,32,128]{2,1,0:T(8,128)(2,1)S(1)} all-to-all(bf16[16,32,128]{2,1,0:T(8,128)(2,1)S(1)} %bitcast.15), channel_id=1, replica_groups={{11,10,9,8,15,14,13,12,3,2,1,16,7,6,5,4},{27,26,25,24,31,30,29,28,19,18..., dimensions={0} | all-to-all | bytes 262144 | tf_op jit(solution)/shard_map/all_to_all | solution.py:129
  30.6 0.7 %shard_map.66 = bf16[2,16,2,8,128]{4,3,2,1,0:T(8,128)(2,1)} custom-call(bf16[16,2,2,8,128]{4,3,2,1,0:T(8,128)(2,1)S(1)} %bitcast.16), custom_call_target="tpu_custom_call" | custom-call | tf_op jit(solution)/shard_map/pallas_call | solution.py:165
Async XLA Ops:
  17.9 1.7 %collective-permute-start = (bf16[16,96,128]{2,1,0:T(8,128)(2,1)S(1)}, bf16[16,96,128]{2,1,0:T(8,128)(2,1)S(1)}, u32[]{:S(2)}, u32[]{:S(2)}) collective-permute-start(bf16[16,96,128]{2,1,0:T(8,128)(2,1)S(1)} %all_to_all.10.own_ref), channel_id=1, source_target_pairs={{0,16},{16,0},{1,17},{17,1},{2,18},{18,2},{3,19},{19,3},{4,20},{20... | collective-permute-start | bytes 1179656 | tf_op jit(solution)/shard_map/ppermute | solution.py:157

commit v7 on v6

--- a/solution.py
+++ b/solution.py
@@ -34,14 +34,16 @@
     width = gate_block.shape[1]
     place = lax.axis_index("ctx") ^ FIRST
     columns = pl.ds(pl.multiple_of(place * width, width), width)
-    pairs = [(levels_ref, levels), (ids_ref, ids), (gate_ref.at[:, columns], gate_block)]
+    pairs = []
     for part, ref in enumerate((query_ref, key_ref, value_ref)):
         for tile in range(ref.shape[0]):
             pairs.append((ref.at[tile], packed_ref.at[:, part, :, tile]))
+    count = len(pairs)
+    pairs += [(levels_ref, levels), (ids_ref, ids), (gate_ref.at[:, columns], gate_block)]
     fetches = [pltpu.make_async_copy(*pair, sems.at[i]) for i, pair in enumerate(pairs)]
     for fetch in fetches:
         fetch.start()
-    for fetch in fetches[:3]:
+    for fetch in fetches[count:]:
         fetch.wait()
     own = own_team()
     other = 1 - own
@@ -62,7 +64,7 @@
         jnp.where(key_swapped, 0.0, crossed),
     ]
     side_ref[pl.ds(0, 6), :] = jnp.concatenate([gate(other), gate(own), *masks], axis=0)
-    for fetch in fetches[3:]:
+    for fetch in fetches[:count]:
         fetch.wait()
 
 
@@ -89,13 +91,15 @@
     scores = [
         [dot(tokens(other_ref, 0, head), tokens(ref, 1, head), (1, 1)) for ref in refs] for head in range(pair)
     ]
-    summed = []
+    weights = []
     for head in range(pair):
         blocks = [masked(score, side) for side, score in enumerate(scores[head])]
         peak = jnp.max(jnp.maximum(*blocks), axis=1, keepdims=True)
-        weights = [jnp.exp2((block - peak) * factor).astype(jnp.bfloat16) for block in blocks]
+        weights.append([jnp.exp2((block - peak) * factor).astype(jnp.bfloat16) for block in blocks])
+    summed = []
+    for head in range(pair):
         values = [jnp.concatenate([tokens(ref, 2, head), ones], axis=1) for ref in refs]
-        summed.append(sum(dot(weight, value, (1, 0)) for weight, value in zip(weights, values)))
+        summed.append(sum(dot(weight, value, (1, 0)) for weight, value in zip(weights[head], values)))
     for head in range(pair):
         attended = (summed[head][:, :HEAD] / summed[head][:, HEAD:]).astype(jnp.bfloat16).astype(jnp.float32)
         gates = [side_ref[kind : kind + 1, head * HEAD : (head + 1) * HEAD] for kind in range(2)]

time: 31.5 us -> 31.5 us (level)
  no operation moved by 1% of the time
where the time goes in v7:
time: 31.5 us; the launch traced here: 31.2 us
  blocking collectives  27.1 us (86%)
  Pallas kernels  2.39 us (8%)
  waiting for transfers between devices  1.72 us (5%)
    all_to_all x2, blocking collectives, exchanged(): lax.all_to_all(chunks, ('group', 'ctx'), split_axis=0, concat_axis=0, til...  27.1 us
    ppermute x1, waiting for transfers between devices, local(): other = lax.ppermute(own, 'group', [(0, 1), (1, 0)])  1.72 us
    pallas_call x1, Pallas kernels, local(): pl.pallas_call(pack_kernel, out_shape=[pltpu.VMEM((members, 3, pair, tile...  1.07 us
    pallas_call x1, Pallas kernels, local(): pl.pallas_call(unpack_kernel, out_shape=pltpu.HBM((tiles, members, pair,...  0.67 us
    pallas_call x1, Pallas kernels, local(): pl.pallas_call(attend_kernel, out_shape=pltpu.VMEM((members, pair, rows,...  0.65 us
  transfers between devices with their start and end apart: 1, of which 1 were waited for; matrix products, arithmetic and copies ran while one was open for 0% of the time, Pallas kernels for 0%

profile of v7, /device:TPU:1, one launch (start us, length us, event | category | flops | bytes accessed | tf_op | source)
XLA Modules:
  0.0 31.2 jit_solution(3916469313514192440)
XLA Ops:
  0.0 1.1 %shard_map.64 = (bf16[16,3,2,2,8,128]{5,4,3,2,1,0:T(8,128)(2,1)S(1)}, f32[8,256]{1,0:T(8,128)S(1)}) custom-call(s32[2]{0:T(128)} %levels_ref.1, s32[2]{0:T(128)} %ids_ref.1, f32[32,4096]{1,0:T(8,128)} %gate_ref.1, bf16[2,16,2,8,128]{4,3,2,1,0:T(8,128)(2,1)} %bitcast.18, bf16[2,16,2,8,128]{4,3,2,1,0:T(8,128)(2,1)} %bitcast.19, ...), custom_call_target="tpu_custom_call" | custom-call | tf_op jit(solution)/shard_map/pallas_call | solution.py:145
  1.1 16.8 %all_to_all.10.own_ref = bf16[16,96,128]{2,1,0:T(8,128)(2,1)S(1)} all-to-all(bf16[16,96,128]{2,1,0:T(8,128)(2,1)S(1)} %bitcast.17), channel_id=1, replica_groups={{11,10,9,8,15,14,13,12,3,2,1,16,7,6,5,4},{27,26,25,24,31,30,29,28,19,18..., dimensions={0} | all-to-all | bytes 786432 | tf_op jit(solution)/shard_map/all_to_all | solution.py:133
  17.9 0.0 collective-permute-start
  17.9 1.7 %collective-permute-done.other_ref = bf16[16,96,128]{2,1,0:T(8,128)(2,1)S(1)} collective-permute-done((bf16[16,96,128]{2,1,0:T(8,128)(2,1)S(1)}, bf16[16,96,128]{2,1,0:T(8,128)(2,1)S(1)}, u32[]{:S(2)}, u32[]{:S(2)}) %collective-permute-start) | collective-permute-done | bytes 393248 | tf_op jit(solution)/shard_map/ppermute | solution.py:161
  19.6 0.7 %shard_map.65 = bf16[16,2,16,128]{3,2,1,0:T(8,128)(2,1)S(1)} custom-call(f32[8,256]{1,0:T(8,128)S(1)} %get-tuple-element.7.side_ref, bf16[16,96,128]{2,1,0:T(8,128)(2,1)S(1)} %all_to_all.10.own_ref, bf16[16,96,128]{2,1,0:T(8,128)(2,1)S(1)} %collective-permute-done.other_ref), custom_call_target="tpu_custom_call" | custom-call | tf_op jit(solution)/shard_map/pallas_call | solution.py:162
  20.3 10.3 %all_to_all.11 = bf16[16,32,128]{2,1,0:T(8,128)(2,1)S(1)} all-to-all(bf16[16,32,128]{2,1,0:T(8,128)(2,1)S(1)} %bitcast.15), channel_id=1, replica_groups={{11,10,9,8,15,14,13,12,3,2,1,16,7,6,5,4},{27,26,25,24,31,30,29,28,19,18..., dimensions={0} | all-to-all | bytes 262144 | tf_op jit(solution)/shard_map/all_to_all | solution.py:133
  30.6 0.7 %shard_map.66 = bf16[2,16,2,8,128]{4,3,2,1,0:T(8,128)(2,1)} custom-call(bf16[16,2,2,8,128]{4,3,2,1,0:T(8,128)(2,1)S(1)} %bitcast.16), custom_call_target="tpu_custom_call" | custom-call | tf_op jit(solution)/shard_map/pallas_call | solution.py:169
Async XLA Ops:
  17.9 1.7 %collective-permute-start = (bf16[16,96,128]{2,1,0:T(8,128)(2,1)S(1)}, bf16[16,96,128]{2,1,0:T(8,128)(2,1)S(1)}, u32[]{:S(2)}, u32[]{:S(2)}) collective-permute-start(bf16[16,96,128]{2,1,0:T(8,128)(2,1)S(1)} %all_to_all.10.own_ref), channel_id=1, source_target_pairs={{0,16},{16,0},{1,17},{17,1},{2,18},{18,2},{3,19},{19,3},{4,20},{20... | collective-permute-start | bytes 1179656 | tf_op jit(solution)/shard_map/ppermute | solution.py:161

commit v8 on v7

--- a/solution.py
+++ b/solution.py
@@ -25,6 +25,10 @@
     for member in SWAPPED:
         team = jnp.where(lax.axis_index("ctx") == member, 1 - team, team)
     return team
+
+
+def halves(places):
+    return [pl.ds(start, places // 2) for start in (0, places // 2)]
 
 
 def pack_kernel(
@@ -37,7 +41,8 @@
     pairs = []
     for part, ref in enumerate((query_ref, key_ref, value_ref)):
         for tile in range(ref.shape[0]):
-            pairs.append((ref.at[tile], packed_ref.at[:, part, :, tile]))
+            for half in halves(packed_ref.shape[0]):
+                pairs.append((ref.at[tile, half], packed_ref.at[half, part, :, tile]))
     count = len(pairs)
     pairs += [(levels_ref, levels), (ids_ref, ids), (gate_ref.at[:, columns], gate_block)]
     fetches = [pltpu.make_async_copy(*pair, sems.at[i]) for i, pair in enumerate(pairs)]
@@ -108,10 +113,11 @@
 
 
 def unpack_kernel(heads_ref, out_ref, sems):
-    copies = [
-        pltpu.make_async_copy(heads_ref.at[:, :, tile], out_ref.at[tile], sems.at[tile])
-        for tile in range(out_ref.shape[0])
+    tiles, places = out_ref.shape[:2]
+    pairs = [
+        (heads_ref.at[half, :, tile], out_ref.at[tile, half]) for tile in range(tiles) for half in halves(places)
     ]
+    copies = [pltpu.make_async_copy(*pair, sems.at[i]) for i, pair in enumerate(pairs)]
     for copy in copies:
         copy.start()
     for copy in copies:
@@ -154,7 +160,7 @@
             pltpu.SMEM(noise_levels.shape, jnp.int32),
             pltpu.SMEM(group_ids.shape, jnp.int32),
             pltpu.VMEM((gate_table.shape[0], pair * HEAD), jnp.float32),
-            pltpu.SemaphoreType.DMA((3 + 3 * tiles,)),
+            pltpu.SemaphoreType.DMA((3 + 6 * tiles,)),
         ],
     )(*(pltpu.with_memory_space_constraint(source, pltpu.HBM) for source in sources))
     own = exchanged(packed.reshape(members, 3 * pair * rows, HEAD))
@@ -171,7 +177,7 @@
         out_shape=pltpu.HBM((tiles, members, pair, TILE, HEAD), jnp.bfloat16),
         in_specs=[whole],
         out_specs=hbm,
-        scratch_shapes=[pltpu.SemaphoreType.DMA((tiles,))],
+        scratch_shapes=[pltpu.SemaphoreType.DMA((2 * tiles,))],
     )(in_vmem(returned.reshape(members, pair, tiles, TILE, HEAD)))
     return handed.transpose(0, 3, 1, 2, 4).reshape(rows, HEADS * HEAD)
 

time: 31.5 us -> 31.6 us (level)
  no operation moved by 1% of the time
where the time goes in v8:
time: 31.6 us; the launch traced here: 31.3 us
  blocking collectives  27.1 us (86%)
  Pallas kernels  2.45 us (8%)
  waiting for transfers between devices  1.72 us (5%)
    all_to_all x2, blocking collectives, exchanged(): lax.all_to_all(chunks, ('group', 'ctx'), split_axis=0, concat_axis=0, til...  27.1 us
    ppermute x1, waiting for transfers between devices, local(): other = lax.ppermute(own, 'group', [(0, 1), (1, 0)])  1.72 us
    pallas_call x1, Pallas kernels, local(): pl.pallas_call(pack_kernel, out_shape=[pltpu.VMEM((members, 3, pair, tile...  1.12 us
    pallas_call x1, Pallas kernels, local(): pl.pallas_call(unpack_kernel, out_shape=pltpu.HBM((tiles, members, pair,...  0.68 us
    pallas_call x1, Pallas kernels, local(): pl.pallas_call(attend_kernel, out_shape=pltpu.VMEM((members, pair, rows,...  0.65 us
  transfers between devices with their start and end apart: 1, of which 1 were waited for; matrix products, arithmetic and copies ran while one was open for 0% of the time, Pallas kernels for 0%

profile of v8, /device:TPU:1, one launch (start us, length us, event | category | flops | bytes accessed | tf_op | source)
XLA Modules:
  0.0 31.3 jit_solution(8155918688419453720)
XLA Ops:
  0.0 1.1 %shard_map.64 = (bf16[16,3,2,2,8,128]{5,4,3,2,1,0:T(8,128)(2,1)S(1)}, f32[8,256]{1,0:T(8,128)S(1)}) custom-call(s32[2]{0:T(128)} %levels_ref.1, s32[2]{0:T(128)} %ids_ref.1, f32[32,4096]{1,0:T(8,128)} %gate_ref.1, bf16[2,16,2,8,128]{4,3,2,1,0:T(8,128)(2,1)} %bitcast.18, bf16[2,16,2,8,128]{4,3,2,1,0:T(8,128)(2,1)} %bitcast.19, ...), custom_call_target="tpu_custom_call" | custom-call | tf_op jit(solution)/shard_map/pallas_call | solution.py:151
  1.1 16.8 %all_to_all.10.own_ref = bf16[16,96,128]{2,1,0:T(8,128)(2,1)S(1)} all-to-all(bf16[16,96,128]{2,1,0:T(8,128)(2,1)S(1)} %bitcast.17), channel_id=1, replica_groups={{11,10,9,8,15,14,13,12,3,2,1,16,7,6,5,4},{27,26,25,24,31,30,29,28,19,18..., dimensions={0} | all-to-all | bytes 786432 | tf_op jit(solution)/shard_map/all_to_all | solution.py:139
  18.0 0.0 collective-permute-start
  18.0 1.7 %collective-permute-done.other_ref = bf16[16,96,128]{2,1,0:T(8,128)(2,1)S(1)} collective-permute-done((bf16[16,96,128]{2,1,0:T(8,128)(2,1)S(1)}, bf16[16,96,128]{2,1,0:T(8,128)(2,1)S(1)}, u32[]{:S(2)}, u32[]{:S(2)}) %collective-permute-start) | collective-permute-done | bytes 393248 | tf_op jit(solution)/shard_map/ppermute | solution.py:167
  19.7 0.6 %shard_map.65 = bf16[16,2,16,128]{3,2,1,0:T(8,128)(2,1)S(1)} custom-call(f32[8,256]{1,0:T(8,128)S(1)} %get-tuple-element.7.side_ref, bf16[16,96,128]{2,1,0:T(8,128)(2,1)S(1)} %all_to_all.10.own_ref, bf16[16,96,128]{2,1,0:T(8,128)(2,1)S(1)} %collective-permute-done.other_ref), custom_call_target="tpu_custom_call" | custom-call | tf_op jit(solution)/shard_map/pallas_call | solution.py:168
  20.3 10.3 %all_to_all.11 = bf16[16,32,128]{2,1,0:T(8,128)(2,1)S(1)} all-to-all(bf16[16,32,128]{2,1,0:T(8,128)(2,1)S(1)} %bitcast.15), channel_id=1, replica_groups={{11,10,9,8,15,14,13,12,3,2,1,16,7,6,5,4},{27,26,25,24,31,30,29,28,19,18..., dimensions={0} | all-to-all | bytes 262144 | tf_op jit(solution)/shard_map/all_to_all | solution.py:139
  30.6 0.7 %shard_map.66 = bf16[2,16,2,8,128]{4,3,2,1,0:T(8,128)(2,1)} custom-call(bf16[16,2,2,8,128]{4,3,2,1,0:T(8,128)(2,1)S(1)} %bitcast.16), custom_call_target="tpu_custom_call" | custom-call | tf_op jit(solution)/shard_map/pallas_call | solution.py:175
Async XLA Ops:
  18.0 1.7 %collective-permute-start = (bf16[16,96,128]{2,1,0:T(8,128)(2,1)S(1)}, bf16[16,96,128]{2,1,0:T(8,128)(2,1)S(1)}, u32[]{:S(2)}, u32[]{:S(2)}) collective-permute-start(bf16[16,96,128]{2,1,0:T(8,128)(2,1)S(1)} %all_to_all.10.own_ref), channel_id=1, source_target_pairs={{0,16},{16,0},{1,17},{17,1},{2,18},{18,2},{3,19},{19,3},{4,20},{20... | collective-permute-start | bytes 1179656 | tf_op jit(solution)/shard_map/ppermute | solution.py:167

commit v9 on v7

--- a/solution.py
+++ b/solution.py
@@ -73,8 +73,13 @@
     group_rows = members * rows
     factor = LOG2_E / HEAD**0.5
     swapped = [place ^ FIRST in SWAPPED for place in range(members)]
-    cuts = [0, *(place for place in range(1, members) if swapped[place] != swapped[place - 1]), members]
-    runs = [(slice(start * rows, stop * rows), swapped[start]) for start, stop in zip(cuts, cuts[1:])]
+    half = members // 2
+    starts = [(head, first) for head in range(pair) for first in (0, half)]
+
+    def runs_from(first):
+        inner = [cut for cut in range(1, half) if swapped[first + cut] != swapped[first + cut - 1]]
+        cuts = [0, *inner, half]
+        return [(slice(i * rows, j * rows), swapped[first + i]) for i, j in zip(cuts, cuts[1:])]
 
     def tokens(ref, part, head):
         return ref[:, pl.ds((part * pair + head) * rows, rows), :].reshape(group_rows, HEAD)
@@ -82,29 +87,31 @@
     def dot(a, b, contract):
         return lax.dot_general(a, b, ((contract[:1], contract[1:]), ((), ())), preferred_element_type=jnp.float32)
 
-    def masked(score, side):
+    def masked(score, side, first):
         masks = [side_ref[2 + 2 * kind + side : 3 + 2 * kind + side, :] for kind in range(2)]
-        return jnp.concatenate([score[run] + masks[kind] for run, kind in runs], axis=0)
+        return jnp.concatenate([score[run] + masks[kind] for run, kind in runs_from(first)], axis=0)
 
     ones = jnp.ones((group_rows, HEAD), jnp.bfloat16)
     refs = (own_ref, other_ref)
+    queries = [tokens(other_ref, 0, head) for head in range(pair)]
     scores = [
-        [dot(tokens(other_ref, 0, head), tokens(ref, 1, head), (1, 1)) for ref in refs] for head in range(pair)
+        [dot(queries[head][first * rows : (first + half) * rows], tokens(ref, 1, head), (1, 1)) for ref in refs]
+        for head, first in starts
     ]
     weights = []
-    for head in range(pair):
-        blocks = [masked(score, side) for side, score in enumerate(scores[head])]
+    for (head, first), score in zip(starts, scores):
+        blocks = [masked(block, side, first) for side, block in enumerate(score)]
         peak = jnp.max(jnp.maximum(*blocks), axis=1, keepdims=True)
         weights.append([jnp.exp2((block - peak) * factor).astype(jnp.bfloat16) for block in blocks])
     summed = []
-    for head in range(pair):
+    for (head, first), weight in zip(starts, weights):
         values = [jnp.concatenate([tokens(ref, 2, head), ones], axis=1) for ref in refs]
-        summed.append(sum(dot(weight, value, (1, 0)) for weight, value in zip(weights[head], values)))
-    for head in range(pair):
-        attended = (summed[head][:, :HEAD] / summed[head][:, HEAD:]).astype(jnp.bfloat16).astype(jnp.float32)
+        summed.append(sum(dot(w, value, (1, 0)) for w, value in zip(weight, values)))
+    for (head, first), total in zip(starts, summed):
+        attended = (total[:, :HEAD] / total[:, HEAD:]).astype(jnp.bfloat16).astype(jnp.float32)
         gates = [side_ref[kind : kind + 1, head * HEAD : (head + 1) * HEAD] for kind in range(2)]
-        done = jnp.concatenate([attended[run] * gates[kind] for run, kind in runs], axis=0).astype(jnp.bfloat16)
-        out_ref[:, head] = done.reshape(members, rows, HEAD)
+        done = jnp.concatenate([attended[run] * gates[kind] for run, kind in runs_from(first)], axis=0)
+        out_ref[pl.ds(first, half), head] = done.astype(jnp.bfloat16).reshape(half, rows, HEAD)
 
 
 def unpack_kernel(heads_ref, out_ref, sems):

time: 31.5 us -> 31.4 us (level)
  no operation moved by 1% of the time
where the time goes in v9:
time: 31.4 us; the launch traced here: 31.2 us
  blocking collectives  27.1 us (86%)
  Pallas kernels  2.36 us (8%)
  waiting for transfers between devices  1.72 us (5%)
    all_to_all x2, blocking collectives, exchanged(): lax.all_to_all(chunks, ('group', 'ctx'), split_axis=0, concat_axis=0, til...  27.1 us
    ppermute x1, waiting for transfers between devices, local(): other = lax.ppermute(own, 'group', [(0, 1), (1, 0)])  1.72 us
    pallas_call x1, Pallas kernels, local(): pl.pallas_call(pack_kernel, out_shape=[pltpu.VMEM((members, 3, pair, tile...  1.07 us
    pallas_call x1, Pallas kernels, local(): pl.pallas_call(unpack_kernel, out_shape=pltpu.HBM((tiles, members, pair,...  0.67 us
  transfers between devices with their start and end apart: 1, of which 1 were waited for; matrix products, arithmetic and copies ran while one was open for 0% of the time, Pallas kernels for 0%

profile of v9, /device:TPU:1, one launch (start us, length us, event | category | flops | bytes accessed | tf_op | source)
XLA Modules:
  0.0 31.2 jit_solution(14027623177910986920)
XLA Ops:
  0.0 1.1 %shard_map.64 = (bf16[16,3,2,2,8,128]{5,4,3,2,1,0:T(8,128)(2,1)S(1)}, f32[8,256]{1,0:T(8,128)S(1)}) custom-call(s32[2]{0:T(128)} %levels_ref.1, s32[2]{0:T(128)} %ids_ref.1, f32[32,4096]{1,0:T(8,128)} %gate_ref.1, bf16[2,16,2,8,128]{4,3,2,1,0:T(8,128)(2,1)} %bitcast.18, bf16[2,16,2,8,128]{4,3,2,1,0:T(8,128)(2,1)} %bitcast.19, ...), custom_call_target="tpu_custom_call" | custom-call | tf_op jit(solution)/shard_map/pallas_call | solution.py:152
  1.1 16.8 %all_to_all.10.own_ref = bf16[16,96,128]{2,1,0:T(8,128)(2,1)S(1)} all-to-all(bf16[16,96,128]{2,1,0:T(8,128)(2,1)S(1)} %bitcast.17), channel_id=1, replica_groups={{11,10,9,8,15,14,13,12,3,2,1,16,7,6,5,4},{27,26,25,24,31,30,29,28,19,18..., dimensions={0} | all-to-all | bytes 786432 | tf_op jit(solution)/shard_map/all_to_all | solution.py:140
  17.9 0.0 collective-permute-start
  17.9 1.7 %collective-permute-done.other_ref = bf16[16,96,128]{2,1,0:T(8,128)(2,1)S(1)} collective-permute-done((bf16[16,96,128]{2,1,0:T(8,128)(2,1)S(1)}, bf16[16,96,128]{2,1,0:T(8,128)(2,1)S(1)}, u32[]{:S(2)}, u32[]{:S(2)}) %collective-permute-start) | collective-permute-done | bytes 393248 | tf_op jit(solution)/shard_map/ppermute | solution.py:168
  19.6 0.6 %shard_map.65 = bf16[16,2,16,128]{3,2,1,0:T(8,128)(2,1)S(1)} custom-call(f32[8,256]{1,0:T(8,128)S(1)} %get-tuple-element.7.side_ref, bf16[16,96,128]{2,1,0:T(8,128)(2,1)S(1)} %all_to_all.10.own_ref, bf16[16,96,128]{2,1,0:T(8,128)(2,1)S(1)} %collective-permute-done.other_ref), custom_call_target="tpu_custom_call" | custom-call | tf_op jit(solution)/shard_map/pallas_call | solution.py:169
  20.3 10.3 %all_to_all.11 = bf16[16,32,128]{2,1,0:T(8,128)(2,1)S(1)} all-to-all(bf16[16,32,128]{2,1,0:T(8,128)(2,1)S(1)} %bitcast.15), channel_id=1, replica_groups={{11,10,9,8,15,14,13,12,3,2,1,16,7,6,5,4},{27,26,25,24,31,30,29,28,19,18..., dimensions={0} | all-to-all | bytes 262144 | tf_op jit(solution)/shard_map/all_to_all | solution.py:140
  30.5 0.7 %shard_map.66 = bf16[2,16,2,8,128]{4,3,2,1,0:T(8,128)(2,1)} custom-call(bf16[16,2,2,8,128]{4,3,2,1,0:T(8,128)(2,1)S(1)} %bitcast.16), custom_call_target="tpu_custom_call" | custom-call | tf_op jit(solution)/shard_map/pallas_call | solution.py:176
Async XLA Ops:
  17.9 1.7 %collective-permute-start = (bf16[16,96,128]{2,1,0:T(8,128)(2,1)S(1)}, bf16[16,96,128]{2,1,0:T(8,128)(2,1)S(1)}, u32[]{:S(2)}, u32[]{:S(2)}) collective-permute-start(bf16[16,96,128]{2,1,0:T(8,128)(2,1)S(1)} %all_to_all.10.own_ref), channel_id=1, source_target_pairs={{0,16},{16,0},{1,17},{17,1},{2,18},{18,2},{3,19},{19,3},{4,20},{20... | collective-permute-start | bytes 1179656 | tf_op jit(solution)/shard_map/ppermute | solution.py:168
